TPU v7x, 512 devices: a whole 4x4x16 slice. The times are simulated.
512 devices in a mesh: scan: 128 (over x, z, core), mode: 4 (over y).
Axes of the slice: x: 4, y: 4, z: 16, core: 2. Of those that a mesh axis runs over, the one named last changes fastest.
Arguments:
- object_field: float32 [2, 12288, 1536], P(None, 'scan', 'mode'), may hold values from -6 to 6
- probe: float32 [4, 2, 256, 256], P('mode'), may hold values from -6 to 6
- measured: float32 [128, 256, 256], P('scan'), may hold values from 0.5 to 8
- positions: int32 [128, 2], P('scan'), may hold values from -96 to 12128, as said below
Outputs:
- new_object: float32 [2, 12288, 1536], P(None, 'scan', 'mode')
- new_probe: float32 [4, 2, 256, 256], P('mode')
Inputs may be any that keep to these rules, and one draw needn't show every extreme that they name: `positions`: A pattern held at scan index s has its corner row between s * 96 - 96 and s * 96 + 2 * 96 - 256, and its corner column between 0 and 1280; some pattern sits at each end of the row band.
All inputs are finite; a program needn't handle non-finite values.
Results may differ from a plain program's by a relative error of at most 0.0003.
Values sent between devices are 32-bit elements; how exact they have to be, the bound alone decides.
A program may use at most 64 MiB of HBM per device.

v0:
```python
import math

import jax
import jax.numpy as jnp
from jax import lax
from jax.sharding import PartitionSpec as P

object_rate = 0.25
precise = lax.Precision.HIGHEST


def extended(cells, sides, width):
    for axis, dim in sides:
        count = lax.axis_size(axis)
        ends = count - 1
        head = lax.slice_in_dim(cells, 0, width, axis=dim)
        tail = lax.slice_in_dim(cells, cells.shape[dim] - width, cells.shape[dim], axis=dim)
        cells = jnp.concatenate(
            [
                lax.ppermute(tail, axis, [(i, (i + 1) % count) for i in range(ends)]),
                cells,
                lax.ppermute(head, axis, [((i + 1) % count, i) for i in range(ends)]),
            ],
            axis=dim,
        )
    return cells


def from_behind(value, axis, steps):
    count = lax.axis_size(axis)
    leading, last = (max(0, -steps), min(count, count - steps))
    return lax.ppermute(value, axis, [(source, source + steps) for source in range(leading, last)])


def twiddle(length):
    index = jnp.arange(length, dtype=jnp.int32)
    product = index[:, None] * index[None, :] % length
    angle = 2.0 * math.pi / length * product.astype(jnp.float32)
    scale = 1.0 / math.sqrt(length)
    return (jnp.cos(angle) * scale, -jnp.sin(angle) * scale)


def left_apply(w_real, w_imag, x_real, x_imag):

    def product(matrix, field):
        return jnp.einsum("ij,kjl->kil", matrix, field, precision=precise)

    return (
        product(w_real, x_real) - product(w_imag, x_imag),
        product(w_real, x_imag) + product(w_imag, x_real),
    )


def right_apply(w_real, w_imag, x_real, x_imag):

    def product(field, matrix):
        return jnp.einsum("kij,jl->kil", field, matrix, precision=precise)

    return (
        product(x_real, w_real) - product(x_imag, w_imag),
        product(x_imag, w_real) + product(x_real, w_imag),
    )


def per_device(object_field, probe, measured, positions):
    tile_rows = object_field.shape[1]
    patch_len = probe.shape[-1]
    pattern_count = measured.shape[0]
    strip_field = lax.all_gather(object_field, "mode", axis=2, tiled=True)
    window = extended(strip_field, (("scan", 1),), tile_rows)
    anchor = lax.axis_index("scan") * tile_rows - tile_rows
    row_start = positions[:, 0] - anchor
    col_start = positions[:, 1]
    zero_index = jnp.zeros((), jnp.int32)

    def extract(row_at, col_at):
        return lax.dynamic_slice(window, (zero_index, row_at, col_at), (2, patch_len, patch_len))

    patches = jax.vmap(extract)(row_start, col_start)
    mode_real = probe[0, 0]
    mode_imag = probe[0, 1]
    wave_real = mode_real * patches[:, 0] - mode_imag * patches[:, 1]
    wave_imag = mode_real * patches[:, 1] + mode_imag * patches[:, 0]
    w_real, w_imag = twiddle(patch_len)
    half_real, half_imag = left_apply(w_real, w_imag, wave_real, wave_imag)
    far_real, far_imag = right_apply(w_real, w_imag, half_real, half_imag)
    far_power = far_real * far_real + far_imag * far_imag
    intensity = lax.psum(far_power, "mode")
    factor = 1.0 - measured / jnp.sqrt(jnp.maximum(intensity, 1.0))
    half_real, half_imag = left_apply(w_real, -w_imag, far_real * factor, far_imag * factor)
    back_real, back_imag = right_apply(w_real, -w_imag, half_real, half_imag)
    term_real = mode_real * back_real + mode_imag * back_imag
    term_imag = mode_real * back_imag - mode_imag * back_real
    probe_real = jnp.sum(patches[:, 0] * back_real + patches[:, 1] * back_imag, axis=0)
    probe_imag = jnp.sum(patches[:, 0] * back_imag - patches[:, 1] * back_real, axis=0)
    probe_local = jnp.stack([probe_real, probe_imag])[None]
    probe_total = lax.psum(probe_local, "scan")
    patterns_all = lax.axis_size("scan") * pattern_count
    new_probe = probe - probe_total / math.sqrt(patterns_all)
    gradient = jnp.zeros(window.shape, jnp.float32)
    stacked = jnp.stack([term_real[0], term_imag[0]])
    corner = (zero_index, row_start[0], col_start[0])
    gradient = lax.dynamic_update_slice(gradient, stacked, corner)
    upper_rim = gradient[:, :tile_rows]
    middle = gradient[:, tile_rows : 2 * tile_rows]
    lower_rim = gradient[:, 2 * tile_rows :]
    strip_grad = middle + from_behind(lower_rim, "scan", 1) + from_behind(upper_rim, "scan", -1)
    tile_grad = lax.psum_scatter(strip_grad, "mode", scatter_dimension=2, tiled=True)
    new_object = object_field - object_rate * tile_grad
    return (new_object, new_probe)


def solution(mesh):
    return jax.shard_map(
        per_device,
        mesh=mesh,
        in_specs=(
            P(None, "scan", "mode"),
            P("mode", None, None, None),
            P("scan", None, None),
            P("scan", None),
        ),
        out_specs=(P(None, "scan", "mode"), P("mode", None, None, None)),
        check_vma=False,
    )
```

profile of v0, /device:TPU:1, one launch (start us, length us, event | category | flops | bytes accessed | tf_op | source)
XLA Modules:
  0.0 542.7 jit_solution(7687527671839172915)
XLA Ops:
  7.9 38.6 %all-gather.2.cloned.1.call-done = f32[2,96,1536]{2,1,0:T(8,128)} async-done(((f32[2,96,384]{2,1,0:T(8,128)}), f32[2,96,1536]{2,1,0:T(8,128)}) %all-gather.2.cloned.1.call-update) | async-done | bytes 1179664 | tf_op jit(solution)/shard_map/all_gather | solution.py:69
  46.6 3.5 collective-permute-start.1
  50.1 3.1 collective-permute-start
  57.1 8.2 %collective-permute-done.1 = f32[2,96,1536]{2,1,0:T(8,128)S(1)} collective-permute-done((f32[2,96,1536]{2,1,0:T(8,128)}, f32[2,96,1536]{2,1,0:T(8,128)S(1)}, u32[]{:S(2)}, u32[]{:S(2)}) %collective-permute-start.1) | collective-permute-done | bytes 1179680 | tf_op jit(solution)/shard_map/ppermute | solution.py:22
  71.1 1.5 fusion.4
  72.6 1.5 fusion.3
  78.5 1.7 convolution_subtract_fusion.2
  82.9 55.5 %all-reduce.3.cloned.1.call-done = f32[1,256,256]{2,1,0:T(8,128)} async-done(((f32[1,256,256]{2,1,0:T(8,128)}), f32[1,256,256]{2,1,0:T(8,128)}) %all-reduce.3.cloned.1.call-update) | async-done | bytes 262160 | tf_op jit(solution)/shard_map/psum | solution.py:88
  139.5 1.5 fusion.11
  141.0 1.5 fusion.15
  142.4 1.5 fusion.1
  143.9 1.5 fusion.2
  149.9 2.4 add_bitcast_fusion
  153.5 7.2 %dynamic_update_slice.3 = f32[2,288,1536]{2,1,0:T(8,128)S(1)} dynamic-update-slice(f32[2,288,1536]{2,1,0:T(8,128)S(1)} %broadcast_in_dim.14, f32[2,256,256]{2,1,0:T(8,128)} %pad_maximum_fusion, s32[]{:T(128)} %constant.42.clone.1, s32[]{:T(128)S(6)} %select_n.52, s32[]{:T(128)S(6)} %select_n.53) | dynamic-update-slice | bytes 1048580 | tf_op jit(solution)/shard_map/dynamic_update_slice | solution.py:103
  160.8 1.6 fusion.116
  162.3 6.1 %collective-permute-start.2 = (f32[2,96,1536]{2,1,0:T(8,128)}, f32[2,96,1536]{2,1,0:T(8,128)}, u32[]{:S(2)}, u32[]{:S(2)}) collective-permute-start(f32[2,96,1536]{2,1,0:T(8,128)} %get-tuple-element.13), channel_id=1, source_target_pairs={{0,4},{4,8},{8,12},{12,16},{16,20},{20,24},{24,28},{28,32},{32,36}... | collective-permute-start | bytes 3538952 | tf_op jit(solution)/shard_map/ppermute | solution.py:32
  168.5 1.9 collective-permute-start.3
  171.3 10.6 %collective-permute-done.2 = f32[2,96,1536]{2,1,0:T(8,128)} collective-permute-done((f32[2,96,1536]{2,1,0:T(8,128)}, f32[2,96,1536]{2,1,0:T(8,128)}, u32[]{:S(2)}, u32[]{:S(2)}) %collective-permute-start.2) | collective-permute-done | bytes 1179680 | tf_op jit(solution)/shard_map/ppermute | solution.py:32
  181.9 4.4 collective-permute-done.3
  186.3 2.9 fusion
  189.3 314.2 %all-reduce.5.cloned.1.call-done = f32[1,2,256,256]{3,2,1,0:T(8,128)} async-done(((f32[1,2,256,256]{3,2,1,0:T(8,128)}), f32[1,2,256,256]{3,2,1,0:T(8,128)}) %all-reduce.5.cloned.1.call-update) | async-done | bytes 524304 | tf_op jit(solution)/shard_map/psum | solution.py:97
  503.5 1.9 multiply_subtract_fusion
  505.4 29.1 %reduce-scatter.2.cloned.1.call-done = f32[2,96,384]{2,1,0:T(8,128)} async-done(((f32[2,96,1536]{2,1,0:T(8,128)}), f32[2,96,384]{2,1,0:T(8,128)}) %reduce-scatter.2.cloned.1.call-update) | async-done | bytes 294928 | tf_op jit(solution)/shard_map/reduce_scatter | solution.py:108
  534.5 1.7 multiply_subtract_fusion.1
  (37 shorter events, 20.6 us)
Async XLA Ops:
  7.2 39.4 %all-gather.2.cloned.1.call-start = ((), (), s32[]{:S(2)}) async-start(), calls=%async_computation.1 | async-start | bytes 1474560 | tf_op jit(solution)/shard_map/all_gather | solution.py:69
  7.9 130.6 %all-reduce.3.cloned.1.call-start = ((), (), s32[]{:S(2)}) async-start(), calls=%async_computation.2 | async-start | bytes 524288 | tf_op jit(solution)/shard_map/psum | solution.py:88
  46.6 18.8 %collective-permute-start.1 = (f32[2,96,1536]{2,1,0:T(8,128)}, f32[2,96,1536]{2,1,0:T(8,128)S(1)}, u32[]{:S(2)}, u32[]{:S(2)}) collective-permute-start(f32[2,96,1536]{2,1,0:T(8,128)} %all-gather.2.cloned.1.call-done), channel_id=1, source_target_pairs={{4,0},{8,4},{12,8},{16,12},{20,16},{24,20},{28,24},{32,28},{36,32}... | collective-permute-start | bytes 3538952 | tf_op jit(solution)/shard_map/ppermute | solution.py:22
  50.1 16.5 %collective-permute-start = (f32[2,96,1536]{2,1,0:T(8,128)}, f32[2,96,1536]{2,1,0:T(8,128)S(1)}, u32[]{:S(2)}, u32[]{:S(2)}) collective-permute-start(f32[2,96,1536]{2,1,0:T(8,128)} %all-gather.2.cloned.1.call-done), channel_id=1, source_target_pairs={{0,4},{4,8},{8,12},{12,16},{16,20},{20,24},{24,28},{28,32},{32,36}... | collective-permute-start | bytes 3538952 | tf_op jit(solution)/shard_map/ppermute | solution.py:20
  66.6 1.4 copy-start
  78.5 60.0 %copy-start.5 = (f32[1,256,256]{2,1,0:T(8,128)S(1)}, f32[1,256,256]{2,1,0:T(8,128)}, u32[]{:S(2)}) copy-start(f32[1,256,256]{2,1,0:T(8,128)} %param.6) | copy-start | bytes 786436
  80.9 422.5 %all-reduce.5.cloned.1.call-start = ((), (), s32[]{:S(2)}) async-start(), calls=%async_computation.4 | async-start | bytes 1048576 | tf_op jit(solution)/shard_map/psum | solution.py:97
  160.7 9.7 %copy-start.3 = (f32[1,256,256]{2,1,0:T(8,128)S(1)}, f32[1,256,256]{2,1,0:T(8,128)}, u32[]{:S(2)}) copy-start(f32[1,256,256]{2,1,0:T(8,128)} %get-tuple-element.15) | copy-start | bytes 786436
  160.8 9.7 %copy-start.4 = (f32[1,256,256]{2,1,0:T(8,128)S(1)}, f32[1,256,256]{2,1,0:T(8,128)}, u32[]{:S(2)}) copy-start(f32[1,256,256]{2,1,0:T(8,128)} %get-tuple-element.16) | copy-start | bytes 786436
  162.3 19.6 %collective-permute-start.2 = (f32[2,96,1536]{2,1,0:T(8,128)}, f32[2,96,1536]{2,1,0:T(8,128)}, u32[]{:S(2)}, u32[]{:S(2)}) collective-permute-start(f32[2,96,1536]{2,1,0:T(8,128)} %get-tuple-element.13), channel_id=1, source_target_pairs={{0,4},{4,8},{8,12},{12,16},{16,20},{20,24},{24,28},{28,32},{32,36}... | collective-permute-start | bytes 3538952 | tf_op jit(solution)/shard_map/ppermute | solution.py:32
  168.5 17.8 %collective-permute-start.3 = (f32[2,96,1536]{2,1,0:T(8,128)}, f32[2,96,1536]{2,1,0:T(8,128)}, u32[]{:S(2)}, u32[]{:S(2)}) collective-permute-start(f32[2,96,1536]{2,1,0:T(8,128)} %get-tuple-element.14), channel_id=1, source_target_pairs={{4,0},{8,4},{12,8},{16,12},{20,16},{24,20},{28,24},{32,28},{36,32}... | collective-permute-start | bytes 3538952 | tf_op jit(solution)/shard_map/ppermute | solution.py:32
  171.3 363.2 %reduce-scatter.2.cloned.1.call-start = ((), (), s32[]{:S(2)}) async-start(), calls=%async_computation.3 | async-start | bytes 1474560 | tf_op jit(solution)/shard_map/reduce_scatter | solution.py:108
  189.2 314.2 %copy-start.1 = (f32[1,2,256,256]{3,2,1,0:T(8,128)S(1)}, f32[1,2,256,256]{3,2,1,0:T(8,128)}, u32[]{:S(2)}) copy-start(f32[1,2,256,256]{3,2,1,0:T(8,128)} %param.5) | copy-start | bytes 1572868
  189.2 345.2 %copy-start.2 = (f32[2,96,384]{2,1,0:T(8,128)S(1)}, f32[2,96,384]{2,1,0:T(8,128)}, u32[]{:S(2)}) copy-start(f32[2,96,384]{2,1,0:T(8,128)} %param.4) | copy-start | bytes 884740
Sparse Core Ops, SparseCore 0:
  10.1 36.4 all-gather.1
  81.1 57.3 all-reduce.2
  171.4 332.0 all-reduce.4
  506.2 28.2 reduce-scatter.1
where the time goes:
time: 544 us; the launch traced here: 543 us
  waiting for transfers between devices  463 us (85%)
  matrix products  24.7 us (5%)
  between operations  18.5 us (3%)
  starting transfers between devices  14.8 us (3%)
  other arithmetic  11.4 us (2%)
  local copies, waits for them, and re-layouts  10.6 us (2%)
    psum x1, waiting for transfers between devices, per_device(): probe_total = lax.psum(probe_local, 'scan')  314 us
    psum x1, waiting for transfers between devices, per_device(): intensity = lax.psum(far_power, 'mode')  55.5 us
    all_gather x1, waiting for transfers between devices, per_device(): strip_field = lax.all_gather(object_field, 'mode', axis=2, tiled=True)  38.6 us
    reduce_scatter x1, waiting for transfers between devices, per_device(): lax.psum_scatter(strip_grad, 'mode', scatter_dimension=2, tiled=True)  29.1 us
    ppermute x2, waiting for transfers between devices, from_behind(): lax.ppermute(value, axis, [(source, source + steps) for source in range(l...  15 us
    dot_general x8, matrix products, product(): return jnp.einsum('kij,jl->kil', field, matrix, precision=precise)  12.8 us
    dot_general x8, matrix products, product(): return jnp.einsum('ij,kjl->kil', matrix, field, precision=precise)  11.9 us
  transfers between devices with their start and end apart: 8, of which 8 were waited for; matrix products, arithmetic and copies ran while one was open for 1% of the time, Pallas kernels for 0%

commit v1 on v0

v1 whole, which is shorter than its diff:
```python
import functools
import math

import jax
import jax.numpy as jnp
import ml_dtypes
import numpy as np
from jax import lax
from jax.experimental import pallas as pl
from jax.experimental.pallas import tpu as pltpu
from jax.sharding import PartitionSpec as P

MESH = pl.DeviceIdType.MESH
F32 = jnp.float32
BF16 = jnp.bfloat16
X_CHIPS = 4
MODES = 4
PATCH = 256
ROWS = 96
COLS = 384
LANES = 128
UNITS = PATCH * PATCH // (8 * LANES)
CHUNK = 64
CHUNKS = PATCH // CHUNK
object_rate = 0.25


def dft_blocks():
    index = np.arange(PATCH)
    angle = 2.0 * math.pi / PATCH * (np.outer(index, index) % PATCH)
    scale = 1.0 / math.sqrt(PATCH)
    real, imag = np.cos(angle) * scale, -np.sin(angle) * scale
    forward = np.block([[real, imag], [-imag, real]])
    parts = []
    for matrix in (forward, forward.T):
        high = matrix.astype(ml_dtypes.bfloat16)
        low = (matrix - high.astype(np.float64)).astype(ml_dtypes.bfloat16)
        parts += [high, low]
    return np.stack(parts)


def split(value):
    high = value.astype(BF16)
    return high, (value - high.astype(F32)).astype(BF16)


def dot(left, right):
    return jnp.dot(left, right, preferred_element_type=F32)


def column_mask(corner, block, shape):
    lane = lax.broadcasted_iota(jnp.int32, shape, 1) + block * LANES
    corner = jnp.broadcast_to(corner, shape)
    return (lane >= corner) & (lane < corner + PATCH)


class Wires:
    def __init__(self, send, recv):
        self.send, self.recv, self.started = send, recv, []

    def put(self, src, dst, scan, mode):
        slot = len(self.started)
        copy = pltpu.make_async_remote_copy(
            src_ref=src,
            dst_ref=dst,
            send_sem=self.send.at[slot],
            recv_sem=self.recv.at[slot],
            device_id=(scan, mode),
            device_id_type=MESH,
        )
        copy.start()
        self.started.append(copy)
        return copy


def kernel(
    scans, chips_x, chips_z,
    pos_ref, obj_ref, probe_ref, meas_ref, dft_ref,
    new_obj_ref, new_probe_ref,
    strip, corners, pick_next, pick_prev, from_prev, from_next,
    patch, wave, stack, far, power, power_a, power_sum, power_b,
    term, term_a, term_sum, term_b, total_term, rim_up, rim_down, grad_prev, grad_next,
    pgrad, pcore, units, units_x, shard, units_z, gathered, gathered_other,
    send_sem, recv_sem,
):
    s = lax.axis_index("scan")
    m = lax.axis_index("mode")
    core = lax.rem(s, 2)
    z = lax.rem(lax.div(s, 2), chips_z)
    x = lax.div(s, 2 * chips_z)
    nxt, prv = lax.rem(s + 1, scans), lax.rem(s + scans - 1, scans)
    m_up, m_dn = lax.rem(m + 1, MODES), lax.rem(m + MODES - 1, MODES)
    pair_a = jnp.where(lax.rem(m, 2) == 0, m + 1, m - 1)
    pair_b = MODES - 1 - m
    other_core = jnp.where(core == 0, s + 1, s - 1)
    wires = Wires(send_sem, recv_sem)

    def at_x(step):
        return (lax.rem(x + step, chips_x) * chips_z + z) * 2 + core

    def at_z(step):
        return (x * chips_z + lax.rem(z + step, chips_z)) * 2 + core

    partners = [(s, m_up), (s, m_dn), (nxt, m), (prv, m)]
    partners += [(at_x(step), m) for step in range(1, chips_x)]
    partners += [(at_z(step), m) for step in range(1, chips_z)]
    barrier = pltpu.get_barrier_semaphore()
    for partner in partners:
        pl.semaphore_signal(barrier, inc=1, device_id=partner, device_id_type=MESH)
    pl.semaphore_wait(barrier, len(partners))

    up_re = wires.put(obj_ref.at[0], strip.at[m, 0], s, m_up)
    dn_im = wires.put(obj_ref.at[1], strip.at[m, 1], s, m_dn)
    row_at = pos_ref[0, 0]
    col_at = pos_ref[0, 1]
    corners[1] = jnp.full((8, LANES), col_at, jnp.int32)
    pos_next = wires.put(corners.at[1], corners.at[0], nxt, m)
    pos_prev = wires.put(corners.at[1], corners.at[2], prv, m)
    up_im = wires.put(obj_ref.at[1], strip.at[m, 1], s, m_up)
    dn_re = wires.put(obj_ref.at[0], strip.at[m, 0], s, m_dn)
    strip[m] = obj_ref[...]
    offset = row_at - ROWS * s + ROWS
    turn = jnp.bitwise_and(col_at, PATCH - 1)
    for part in range(2):
        rolled = pltpu.roll(probe_ref[0, part], turn, 1)
        wave[part] = pltpu.roll(rolled, offset, 0)
    pos_next.wait_recv()
    pos_prev.wait_recv()
    up_re.wait_recv()
    fwd_re = wires.put(strip.at[m_dn, 0], strip.at[m_dn, 0], s, m_up)
    dn_im.wait_recv()
    fwd_im = wires.put(strip.at[m_up, 1], strip.at[m_up, 1], s, m_dn)

    def chosen(part, who, half):
        shape = (ROWS, LANES)
        corner = corners[who, 0:1, :]
        picked = jnp.zeros(shape, F32)
        for block in range(half, MODES * COLS // LANES, 2):
            tile, inner = divmod(block, COLS // LANES)
            cells = strip[tile, part, :, inner * LANES : (inner + 1) * LANES]
            picked = jnp.where(column_mask(corner, block, shape), cells, picked)
        return picked

    halos = []
    for part in range(2):
        if part == 0:
            dn_re.wait_recv()
            fwd_re.wait_recv()
        else:
            up_im.wait_recv()
            fwd_im.wait_recv()
        for half in range(2):
            lanes = slice(half * LANES, (half + 1) * LANES)
            pick_next[part, :, lanes] = chosen(part, 2, half)
            pick_prev[part, :, lanes] = chosen(part, 0, half)
        halos.append(wires.put(pick_next.at[part], from_prev.at[part], nxt, m))
        halos.append(wires.put(pick_prev.at[part], from_next.at[part], prv, m))
        for half in range(2):
            lanes = slice(half * LANES, (half + 1) * LANES)
            patch[part, ROWS : 2 * ROWS, lanes] = chosen(part, 1, half)
    for halo in halos:
        halo.wait_recv()
    seam = lax.broadcasted_iota(jnp.int32, (32, PATCH), 0)
    for part in range(2):
        above = jnp.where(s > 0, from_prev[part], 0.0)
        below = jnp.where(s < scans - 1, from_next[part], 0.0)
        patch[part, 0:32] = jnp.where(seam >= offset, above[0:32], below[64:96])
        patch[part, 32:96] = above[32:96]
        patch[part, 192:256] = below[0:64]

    def along_rows(value, which):
        high, low = split(value)
        return dot(high, dft_ref[which]) + dot(low, dft_ref[which]) + dot(high, dft_ref[which + 1])

    def along_columns(rows, which):
        first = dot(dft_ref[which, rows, :], stack[0]) + dot(dft_ref[which, rows, :], stack[1])
        return first + dot(dft_ref[which + 1, rows, :], stack[0])

    def keep(value, rows):
        high, low = split(value)
        for part in range(2):
            lanes = slice(part * PATCH, (part + 1) * PATCH)
            into = slice(part * PATCH + rows.start, part * PATCH + rows.stop)
            stack[0, into] = high[:, lanes]
            stack[1, into] = low[:, lanes]

    slices = [slice(i * CHUNK, (i + 1) * CHUNK) for i in range(CHUNKS)]
    for rows in slices:
        p_re, p_im = wave[0, rows], wave[1, rows]
        o_re, o_im = patch[0, rows], patch[1, rows]
        exit_wave = jnp.concatenate([p_re * o_re - p_im * o_im, p_re * o_im + p_im * o_re], axis=1)
        keep(along_rows(exit_wave, 0), rows)

    def route(i):
        return (pair_a, pair_b) if i % 2 == 0 else (pair_b, pair_a)

    hops = []
    for i, rows in enumerate(slices):
        f_re = along_columns(rows, 2)
        f_im = along_columns(slice(PATCH + rows.start, PATCH + rows.stop), 2)
        far[0, rows] = f_re
        far[1, rows] = f_im
        power[rows] = f_re * f_re + f_im * f_im
        hops.append(wires.put(power.at[rows], power_a.at[rows], s, route(i)[0]))
    more = []
    for i, rows in enumerate(slices):
        hops[i].wait_recv()
        power_sum[rows] = power[rows] + power_a[rows]
        more.append(wires.put(power_sum.at[rows], power_b.at[rows], s, route(i)[1]))
    for i, rows in enumerate(slices):
        more[i].wait_recv()
        intensity = power_sum[rows] + power_b[rows]
        factor = 1.0 - meas_ref[0, rows] / jnp.sqrt(jnp.maximum(intensity, 1.0))
        scaled = jnp.concatenate([far[0, rows] * factor, far[1, rows] * factor], axis=1)
        keep(along_rows(scaled, 2), rows)

    hops = []
    for i, rows in enumerate(slices):
        b_re = along_columns(rows, 0)
        b_im = along_columns(slice(PATCH + rows.start, PATCH + rows.stop), 0)
        p_re, p_im = wave[0, rows], wave[1, rows]
        term[0, rows] = p_re * b_re + p_im * b_im
        term[1, rows] = p_re * b_im - p_im * b_re
        hops.append(wires.put(term.at[:, rows], term_a.at[:, rows], s, route(i)[0]))
        o_re, o_im = patch[0, rows], patch[1, rows]
        pgrad[0, rows] = o_re * b_re + o_im * b_im
        pgrad[1, rows] = o_re * b_im - o_im * b_re

    for part in range(2):
        turned = pltpu.roll(pgrad[part], PATCH - offset, 0)
        pgrad[part] = pltpu.roll(turned, PATCH - turn, 1)
    to_core = wires.put(pgrad.at[1 - core], pcore, other_core, m)

    more = []
    for i, rows in enumerate(slices[:2]):
        hops[i].wait_recv()
        term_sum[:, rows] = term[:, rows] + term_a[:, rows]
        more.append(wires.put(term_sum.at[:, rows], term_b.at[:, rows], s, route(i)[1]))

    def unit_slices(unit):
        return slice(unit // 2 * 8, unit // 2 * 8 + 8), slice(unit % 2 * LANES, (unit % 2 + 1) * LANES)

    to_core.wait_recv()
    own = pgrad.at[core]
    for unit in range(UNITS):
        rows, lanes = unit_slices(unit)
        units[unit] = own[rows, lanes] + pcore[rows, lanes]
    per_x = UNITS // chips_x
    per_z = per_x // chips_z
    to_x = []
    for step in range(1, chips_x):
        there = lax.rem(x + step, chips_x) * per_x
        to_x.append(wires.put(units.at[pl.ds(there, per_x)], units_x.at[step], at_x(step), m))

    for i, rows in list(enumerate(slices))[2:]:
        hops[i].wait_recv()
        term_sum[:, rows] = term[:, rows] + term_a[:, rows]
        more.append(wires.put(term_sum.at[:, rows], term_b.at[:, rows], s, route(i)[1]))

    total = units[pl.ds(x * per_x, per_x)]
    for step in range(1, chips_x):
        to_x[step - 1].wait_recv()
        total = total + units_x[step]
    shard[...] = total
    to_z = []
    for step in range(1, chips_z):
        there = lax.rem(z + step, chips_z) * per_z
        to_z.append(wires.put(shard.at[pl.ds(there, per_z)], units_z.at[step], at_z(step), m))
    total = shard[pl.ds(z * per_z, per_z)]
    for step in range(1, chips_z):
        to_z[step - 1].wait_recv()
        total = total + units_z[step]
    first = x * per_x + z * per_z
    scale = 1.0 / math.sqrt(scans)
    for i in range(per_z):
        unit = first + i
        rows = pl.ds(pl.multiple_of(lax.div(unit, 2) * 8, 8), 8)
        lanes = pl.ds(pl.multiple_of(lax.rem(unit, 2) * LANES, LANES), LANES)
        gathered[unit] = probe_ref[0, core, rows, lanes] - total[i] * scale
    mine = gathered.at[pl.ds(first, per_z)]
    back_z = [wires.put(mine, mine, at_z(step), m) for step in range(1, chips_z)]

    for i, rows in enumerate(slices):
        more[i].wait_recv()
        total_term[:, rows] = term_sum[:, rows] + term_b[:, rows]
    for part in range(2):
        edge = total_term[part, 0:32]
        rim_up[part, 0:32] = jnp.where(seam >= offset, edge, 0.0)
        rim_up[part, 32:96] = total_term[part, 32:96]
        rim_down[part, 0:64] = total_term[part, 192:256]
        rim_down[part, 64:96] = jnp.where(seam < offset, edge, 0.0)
    to_prev = wires.put(rim_up, grad_next, prv, m)
    to_next = wires.put(rim_down, grad_prev, nxt, m)

    for copy in back_z:
        copy.wait_recv()
    mine = gathered.at[pl.ds(x * per_x, per_x)]
    back_x = [wires.put(mine, mine, at_x(step), m) for step in range(1, chips_x)]

    to_prev.wait_recv()
    to_next.wait_recv()
    shape = (ROWS, LANES)
    for inner in range(COLS // LANES):
        block = m * (COLS // LANES) + inner
        lanes = pl.ds(pl.multiple_of(lax.rem(block, 2) * LANES, LANES), LANES)
        masks = [column_mask(corners[who, 0:1, :], block, shape) for who in range(3)]
        for part in range(2):
            above = jnp.where(s > 0, grad_prev[part, :, lanes], 0.0)
            below = jnp.where(s < scans - 1, grad_next[part, :, lanes], 0.0)
            total = jnp.where(masks[1], total_term[part, ROWS : 2 * ROWS, lanes], 0.0)
            total = total + jnp.where(masks[0], above, 0.0) + jnp.where(masks[2], below, 0.0)
            here = slice(inner * LANES, (inner + 1) * LANES)
            new_obj_ref[part, :, here] = obj_ref[part, :, here] - object_rate * total

    for copy in back_x:
        copy.wait_recv()
    back_core = wires.put(gathered, gathered_other, other_core, m)
    for unit in range(UNITS):
        rows, lanes = unit_slices(unit)
        new_probe_ref[0, core, rows, lanes] = gathered[unit]
    back_core.wait_recv()
    for unit in range(UNITS):
        rows, lanes = unit_slices(unit)
        new_probe_ref[0, 1 - core, rows, lanes] = gathered_other[unit]
    for copy in wires.started:
        copy.wait_send()


def per_device(scans, chips_x, object_field, probe, measured, positions):
    chips_z = scans // (2 * chips_x)
    per_x = UNITS // chips_x
    per_z = per_x // chips_z
    wire_count = 12 + 6 * CHUNKS // 2 + 4 + 2 + 2 * (chips_x + chips_z) + CHUNKS
    field = pltpu.VMEM((2, PATCH, PATCH), F32)
    plane = pltpu.VMEM((PATCH, PATCH), F32)
    rim = pltpu.VMEM((2, ROWS, PATCH), F32)
    vmem = pl.BlockSpec(memory_space=pltpu.VMEM)
    return pl.pallas_call(
        functools.partial(kernel, scans, chips_x, chips_z),
        out_shape=(
            jax.ShapeDtypeStruct(object_field.shape, F32),
            jax.ShapeDtypeStruct(probe.shape, F32),
        ),
        in_specs=[pl.BlockSpec(memory_space=pltpu.SMEM)] + [vmem] * 4,
        out_specs=(vmem, vmem),
        scratch_shapes=[
            pltpu.VMEM((MODES, 2, ROWS, COLS), F32),
            pltpu.VMEM((3, 8, LANES), jnp.int32),
            rim, rim, rim, rim,
            field, field,
            pltpu.VMEM((2, 2 * PATCH, PATCH), BF16),
            field,
            plane, plane, plane, plane,
            field, field, field, field, field,
            rim, rim, rim, rim,
            field, plane,
            pltpu.VMEM((UNITS, 8, LANES), F32),
            pltpu.VMEM((chips_x, per_x, 8, LANES), F32),
            pltpu.VMEM((per_x, 8, LANES), F32),
            pltpu.VMEM((chips_z, per_z, 8, LANES), F32),
            pltpu.VMEM((UNITS, 8, LANES), F32),
            pltpu.VMEM((UNITS, 8, LANES), F32),
            pltpu.SemaphoreType.DMA((wire_count,)),
            pltpu.SemaphoreType.DMA((wire_count,)),
        ],
        compiler_params=pltpu.CompilerParams(
            collective_id=0, has_side_effects=True, vmem_limit_bytes=48 << 20
        ),
        cost_estimate=pl.CostEstimate(flops=1 << 31, bytes_accessed=4 << 20, transcendentals=0),
    )(positions, object_field, probe, measured, jnp.asarray(dft_blocks()))


def solution(mesh):
    return jax.shard_map(
        functools.partial(per_device, mesh.shape["scan"], X_CHIPS),
        mesh=mesh,
        in_specs=(
            P(None, "scan", "mode"),
            P("mode", None, None, None),
            P("scan", None, None),
            P("scan", None),
        ),
        out_specs=(P(None, "scan", "mode"), P("mode", None, None, None)),
        check_vma=False,
    )
```

time: 544 us -> 87.8 us (0.16)
  waiting for transfers between devices: 463 us -> 0 us
  Pallas kernels: 0 us -> 80.2 us
  matrix products: 24.7 us -> 0 us
  between operations: 18.5 us -> 0.65 us
  starting transfers between devices: 14.8 us -> 0 us
  other arithmetic: 11.4 us -> 0 us
    psum x2 -> x0, waiting for transfers between devices: 370 us -> none  [the longest x1 314 us: per_device(): probe_total = lax.psum(probe_local, 'scan')]
    pallas_call x0 -> x1, Pallas kernels: none -> 80.2 us  [per_device(): pl.pallas_call(functools.partial(kernel, scans, chips_x, chips_z), out_sh...]
    all_gather x1 -> x0, waiting for transfers between devices: 38.6 us -> none  [per_device(): strip_field = lax.all_gather(object_field, 'mode', axis=2, tiled=True)]
    reduce_scatter x1 -> x0, waiting for transfers between devices: 29.1 us -> none  [per_device(): lax.psum_scatter(strip_grad, 'mode', scatter_dimension=2, tiled=True)]
    dot_general x16 -> x0, matrix products: 24.7 us -> none  [the longest x8 12.8 us: product(): return jnp.einsum('kij,jl->kil', field, matrix, precision=precise)]
    ppermute x4 -> x0, waiting for transfers between devices: 24.5 us -> none  [the longest x2 15 us: from_behind(): lax.ppermute(value, axis, [(source, source + steps) for source in range(l...]
    ppermute x4 -> x0, starting transfers between devices: 14.7 us -> none  [the longest x2 8.07 us: from_behind(): lax.ppermute(value, axis, [(source, source + steps) for source in range(l...]
    dynamic_update_slice x1 -> x0, local copies, waits for them, and re-layouts: 7.25 us -> none  [per_device(): gradient = lax.dynamic_update_slice(gradient, stacked, corner)]
  transfers between devices with their start and end apart: 8 -> 0, of which waited for: 8 -> 0; matrix products, arithmetic and copies ran while one was open for 1% -> 0% of each run, Pallas kernels for 0% -> 0%
where the time goes in v1:
time: 87.8 us; the launch traced here: 87.6 us
  Pallas kernels  80.2 us (91%)
  local copies, waits for them, and re-layouts  6.7 us (8%)
    pallas_call x1, Pallas kernels, per_device(): pl.pallas_call(functools.partial(kernel, scans, chips_x, chips_z), out_sh...  80.2 us
    unnamed x12, local copies, waits for them, and re-layouts  6.7 us

profile of v1, /device:TPU:1, one launch (start us, length us, event | category | flops | bytes accessed | tf_op | source)
XLA Modules:
  0.0 87.6 jit_solution(352954473417333085)
XLA Ops:
  0.6 0.0 copy-start
  0.6 1.0 %copy-done = f32[1,2,256,256]{3,2,1,0:T(8,128)S(1)} copy-done((f32[1,2,256,256]{3,2,1,0:T(8,128)S(1)}, f32[1,2,256,256]{3,2,1,0:T(8,128)}, u32[]{:S(2)}) %copy-start) | copy-done | bytes 524312
  1.7 0.0 copy-start.1
  1.7 1.0 %copy-done.1 = f32[2,96,384]{2,1,0:T(8,128)S(1)} copy-done((f32[2,96,384]{2,1,0:T(8,128)S(1)}, f32[2,96,384]{2,1,0:T(8,128)}, u32[]{:S(2)}) %copy-start.1) | copy-done | bytes 294936
  2.6 0.0 copy-start.2
  2.6 0.9 %copy-done.2 = f32[1,256,256]{2,1,0:T(8,128)S(1)} copy-done((f32[1,256,256]{2,1,0:T(8,128)S(1)}, f32[1,256,256]{2,1,0:T(8,128)}, u32[]{:S(2)}) %copy-start.2) | copy-done | bytes 262168
  3.6 0.0 copy-start.3
  3.6 0.7 copy-done.3
  4.2 0.0 copy-start.4
  4.2 1.6 %copy-done.4 = bf16[4,512,512]{2,1,0:T(8,128)(2,1)S(1)} copy-done((bf16[4,512,512]{2,1,0:T(8,128)(2,1)S(1)}, bf16[4,512,512]{2,1,0:T(8,128)(2,1)}, u32[]{:S(2)}) %copy-start.4) | copy-done | bytes 2097176
  5.8 80.2 %shard_map.68 = (f32[2,96,384]{2,1,0:T(8,128)S(1)}, f32[1,2,256,256]{3,2,1,0:T(8,128)S(1)}) custom-call(s32[1,2]{1,0:T(1,128)S(1)} %copy-done.3, f32[2,96,384]{2,1,0:T(8,128)S(1)} %copy-done.1, f32[1,2,256,256]{3,2,1,0:T(8,128)S(1)} %copy-done, f32[1,256,256]{2,1,0:T(8,128)S(1)} %copy-done.2, bf16[4,512,512]{2,1,0:T(8,128)(2,1)S(1)} %copy-done.4), custom_call_target="tpu_custom_call" | custom-call | flops 2147483648 | bytes 4194304 | tf_op jit(solution)/shard_map/pallas_call | solution.py:338
  86.1 0.7 copy.9
  86.8 0.8 copy.10
Async XLA Ops:
  0.6 1.0 %copy-start = (f32[1,2,256,256]{3,2,1,0:T(8,128)S(1)}, f32[1,2,256,256]{3,2,1,0:T(8,128)}, u32[]{:S(2)}) copy-start(f32[1,2,256,256]{3,2,1,0:T(8,128)} %probe_ref.1) | copy-start | bytes 1572868
  1.7 1.0 %copy-start.1 = (f32[2,96,384]{2,1,0:T(8,128)S(1)}, f32[2,96,384]{2,1,0:T(8,128)}, u32[]{:S(2)}) copy-start(f32[2,96,384]{2,1,0:T(8,128)} %obj_ref.1) | copy-start | bytes 884740
  2.6 0.9 %copy-start.2 = (f32[1,256,256]{2,1,0:T(8,128)S(1)}, f32[1,256,256]{2,1,0:T(8,128)}, u32[]{:S(2)}) copy-start(f32[1,256,256]{2,1,0:T(8,128)} %meas_ref.1) | copy-start | bytes 786436
  3.6 0.7 copy-start.3
  4.2 1.6 %copy-start.4 = (bf16[4,512,512]{2,1,0:T(8,128)(2,1)S(1)}, bf16[4,512,512]{2,1,0:T(8,128)(2,1)}, u32[]{:S(2)}) copy-start(bf16[4,512,512]{2,1,0:T(8,128)(2,1)} %constant.2.clone.dft_ref) | copy-start | bytes 6291460

commit v2 on v1

--- a/solution.py
+++ b/solution.py
@@ -17,6 +17,7 @@
 MODES = 4
 PATCH = 256
 ROWS = 96
+THIRD = 32
 COLS = 384
 LANES = 128
 UNITS = PATCH * PATCH // (8 * LANES)
@@ -25,18 +26,11 @@
 object_rate = 0.25
 
 
-def dft_blocks():
+def dft_parts():
     index = np.arange(PATCH)
     angle = 2.0 * math.pi / PATCH * (np.outer(index, index) % PATCH)
     scale = 1.0 / math.sqrt(PATCH)
-    real, imag = np.cos(angle) * scale, -np.sin(angle) * scale
-    forward = np.block([[real, imag], [-imag, real]])
-    parts = []
-    for matrix in (forward, forward.T):
-        high = matrix.astype(ml_dtypes.bfloat16)
-        low = (matrix - high.astype(np.float64)).astype(ml_dtypes.bfloat16)
-        parts += [high, low]
-    return np.stack(parts)
+    return np.stack([np.cos(angle) * scale, -np.sin(angle) * scale]).astype(np.float32)
 
 
 def split(value):
@@ -50,7 +44,6 @@
 
 def column_mask(corner, block, shape):
     lane = lax.broadcasted_iota(jnp.int32, shape, 1) + block * LANES
-    corner = jnp.broadcast_to(corner, shape)
     return (lane >= corner) & (lane < corner + PATCH)
 
 
@@ -75,13 +68,14 @@
 
 def kernel(
     scans, chips_x, chips_z,
-    pos_ref, obj_ref, probe_ref, meas_ref, dft_ref,
+    pos_ref, obj_ref, probe_hbm, meas_hbm, dft_hbm,
     new_obj_ref, new_probe_ref,
+    probe_ref, meas_ref, dft_ref, row_ops, col_ops,
     strip, corners, pick_next, pick_prev, from_prev, from_next,
     patch, wave, stack, far, power, power_a, power_sum, power_b,
     term, term_a, term_sum, term_b, total_term, rim_up, rim_down, grad_prev, grad_next,
     pgrad, pcore, units, units_x, shard, units_z, gathered, gathered_other,
-    send_sem, recv_sem,
+    send_sem, recv_sem, local_sem,
 ):
     s = lax.axis_index("scan")
     m = lax.axis_index("mode")
@@ -109,72 +103,112 @@
         pl.semaphore_signal(barrier, inc=1, device_id=partner, device_id_type=MESH)
     pl.semaphore_wait(barrier, len(partners))
 
-    up_re = wires.put(obj_ref.at[0], strip.at[m, 0], s, m_up)
-    dn_im = wires.put(obj_ref.at[1], strip.at[m, 1], s, m_dn)
+    def cells_of(tile, part, t):
+        return strip.at[tile, part, t * THIRD : (t + 1) * THIRD]
+
+    def own_cells(part, t):
+        return obj_ref.at[part, t * THIRD : (t + 1) * THIRD]
+
+    up, dn, fwd_up, fwd_dn = {}, {}, {}, {}
+
+    def send_own(t):
+        up[0, t] = wires.put(own_cells(0, t), cells_of(m, 0, t), s, m_up)
+        dn[1, t] = wires.put(own_cells(1, t), cells_of(m, 1, t), s, m_dn)
+        up[1, t] = wires.put(own_cells(1, t), cells_of(m, 1, t), s, m_up)
+        dn[0, t] = wires.put(own_cells(0, t), cells_of(m, 0, t), s, m_dn)
+
+    def forward(t):
+        up[0, t].wait_recv()
+        fwd_up[t] = wires.put(cells_of(m_dn, 0, t), cells_of(m_dn, 0, t), s, m_up)
+        dn[1, t].wait_recv()
+        fwd_dn[t] = wires.put(cells_of(m_up, 1, t), cells_of(m_up, 1, t), s, m_dn)
+
+    send_own(0)
+    locals_ = [
+        pltpu.make_async_copy(src, dst, local_sem.at[i])
+        for i, (src, dst) in enumerate(
+            [(obj_ref, strip.at[m]), (dft_hbm, dft_ref), (probe_hbm, probe_ref), (meas_hbm, meas_ref)]
+        )
+    ]
+    for copy in locals_:
+        copy.start()
     row_at = pos_ref[0, 0]
     col_at = pos_ref[0, 1]
     corners[1] = jnp.full((8, LANES), col_at, jnp.int32)
     pos_next = wires.put(corners.at[1], corners.at[0], nxt, m)
     pos_prev = wires.put(corners.at[1], corners.at[2], prv, m)
-    up_im = wires.put(obj_ref.at[1], strip.at[m, 1], s, m_up)
-    dn_re = wires.put(obj_ref.at[0], strip.at[m, 0], s, m_dn)
-    strip[m] = obj_ref[...]
+    send_own(1)
+    send_own(2)
+    for copy in locals_:
+        copy.wait()
+
+    def transforms():
+        real, imag = dft_ref[0], dft_ref[1]
+        for part, (re, im) in enumerate(zip(split(real), split(imag))):
+            for which, sign in enumerate((im, -im)):
+                row_ops[which, part, 0:PATCH, 0:PATCH] = re
+                row_ops[which, part, 0:PATCH, PATCH:] = sign
+                row_ops[which, part, PATCH:, 0:PATCH] = -sign
+                row_ops[which, part, PATCH:, PATCH:] = re
+                for i in range(CHUNKS):
+                    rows = slice(i * CHUNK, (i + 1) * CHUNK)
+                    at = (4 * i + 2 * part) * CHUNK
+                    col_ops[which, at : at + CHUNK, 0:PATCH] = re[rows]
+                    col_ops[which, at : at + CHUNK, PATCH:] = -sign[rows]
+                    col_ops[which, at + CHUNK : at + 2 * CHUNK, 0:PATCH] = sign[rows]
+                    col_ops[which, at + CHUNK : at + 2 * CHUNK, PATCH:] = re[rows]
+
     offset = row_at - ROWS * s + ROWS
     turn = jnp.bitwise_and(col_at, PATCH - 1)
+    transforms()
+    forward(0)
     for part in range(2):
         rolled = pltpu.roll(probe_ref[0, part], turn, 1)
         wave[part] = pltpu.roll(rolled, offset, 0)
     pos_next.wait_recv()
     pos_prev.wait_recv()
-    up_re.wait_recv()
-    fwd_re = wires.put(strip.at[m_dn, 0], strip.at[m_dn, 0], s, m_up)
-    dn_im.wait_recv()
-    fwd_im = wires.put(strip.at[m_up, 1], strip.at[m_up, 1], s, m_dn)
-
-    def chosen(part, who, half):
-        shape = (ROWS, LANES)
-        corner = corners[who, 0:1, :]
-        picked = jnp.zeros(shape, F32)
-        for block in range(half, MODES * COLS // LANES, 2):
-            tile, inner = divmod(block, COLS // LANES)
-            cells = strip[tile, part, :, inner * LANES : (inner + 1) * LANES]
-            picked = jnp.where(column_mask(corner, block, shape), cells, picked)
-        return picked
-
-    halos = []
-    for part in range(2):
-        if part == 0:
-            dn_re.wait_recv()
-            fwd_re.wait_recv()
-        else:
-            up_im.wait_recv()
-            fwd_im.wait_recv()
-        for half in range(2):
-            lanes = slice(half * LANES, (half + 1) * LANES)
-            pick_next[part, :, lanes] = chosen(part, 2, half)
-            pick_prev[part, :, lanes] = chosen(part, 0, half)
-        halos.append(wires.put(pick_next.at[part], from_prev.at[part], nxt, m))
-        halos.append(wires.put(pick_prev.at[part], from_next.at[part], prv, m))
-        for half in range(2):
-            lanes = slice(half * LANES, (half + 1) * LANES)
-            patch[part, ROWS : 2 * ROWS, lanes] = chosen(part, 1, half)
-    for halo in halos:
-        halo.wait_recv()
-    seam = lax.broadcasted_iota(jnp.int32, (32, PATCH), 0)
-    for part in range(2):
-        above = jnp.where(s > 0, from_prev[part], 0.0)
-        below = jnp.where(s < scans - 1, from_next[part], 0.0)
-        patch[part, 0:32] = jnp.where(seam >= offset, above[0:32], below[64:96])
-        patch[part, 32:96] = above[32:96]
-        patch[part, 192:256] = below[0:64]
+
+    def choose(t):
+        corner = [corners[who] for who in range(3)]
+        blocks = MODES * COLS // LANES
+        for part in range(2):
+            if part == 0:
+                dn[0, t].wait_recv()
+                fwd_up[t].wait_recv()
+            else:
+                up[1, t].wait_recv()
+                fwd_dn[t].wait_recv()
+            for row in range(t * THIRD, (t + 1) * THIRD, 8):
+                rows = slice(row, row + 8)
+                picked = [[jnp.zeros((8, LANES), F32)] * 2 for who in range(3)]
+                for block in range(blocks):
+                    tile, inner = divmod(block, COLS // LANES)
+                    cells = strip[tile, part, rows, inner * LANES : (inner + 1) * LANES]
+                    for who in range(3):
+                        mask = column_mask(corner[who], block, (8, LANES))
+                        picked[who][block % 2] = jnp.where(mask, cells, picked[who][block % 2])
+                for half in range(2):
+                    lanes = slice(half * LANES, (half + 1) * LANES)
+                    pick_prev[part, rows, lanes] = picked[0][half]
+                    patch[part, ROWS + row : ROWS + row + 8, lanes] = picked[1][half]
+                    pick_next[part, rows, lanes] = picked[2][half]
+        rows = slice(t * THIRD, (t + 1) * THIRD)
+        return (
+            wires.put(pick_next.at[:, rows], from_prev.at[:, rows], nxt, m),
+            wires.put(pick_prev.at[:, rows], from_next.at[:, rows], prv, m),
+        )
 
     def along_rows(value, which):
         high, low = split(value)
-        return dot(high, dft_ref[which]) + dot(low, dft_ref[which]) + dot(high, dft_ref[which + 1])
-
-    def along_columns(rows, which):
-        first = dot(dft_ref[which, rows, :], stack[0]) + dot(dft_ref[which, rows, :], stack[1])
-        return first + dot(dft_ref[which + 1, rows, :], stack[0])
+        count = value.shape[0]
+        both = dot(jnp.concatenate([high, low], axis=0), row_ops[which, 0])
+        return both[:count] + both[count:] + dot(high, row_ops[which, 1])
+
+    def along_columns(i, which):
+        at = 4 * CHUNK * i
+        both = dot(col_ops[which, at : at + 4 * CHUNK], stack[0])
+        result = both[: 2 * CHUNK] + both[2 * CHUNK :] + dot(col_ops[which, at : at + 2 * CHUNK], stack[1])
+        return result[:CHUNK], result[CHUNK:]
 
     def keep(value, rows):
         high, low = split(value)
@@ -184,20 +218,50 @@
             stack[0, into] = high[:, lanes]
             stack[1, into] = low[:, lanes]
 
+    def first_stage(*pieces):
+        waves = []
+        for rows in pieces:
+            p_re, p_im = wave[0, rows], wave[1, rows]
+            o_re, o_im = patch[0, rows], patch[1, rows]
+            waves.append(jnp.concatenate([p_re * o_re - p_im * o_im, p_re * o_im + p_im * o_re], axis=1))
+        result = along_rows(jnp.concatenate(waves, axis=0), 0)
+        at = 0
+        for rows in pieces:
+            count = rows.stop - rows.start
+            keep(result[at : at + count], rows)
+            at += count
+
+    halos = [choose(0)]
+    forward(1)
+    halos.append(choose(1))
+    forward(2)
+    halos.append(choose(2))
+    first_stage(slice(ROWS, 2 * ROWS))
+    seam = lax.broadcasted_iota(jnp.int32, (32, PATCH), 0)
+    for halo in halos[:2]:
+        for copy in halo:
+            copy.wait_recv()
+    for part in range(2):
+        patch[part, 192:256] = jnp.where(s < scans - 1, from_next[part, 0:64], 0.0)
+        patch[part, 32:64] = jnp.where(s > 0, from_prev[part, 32:64], 0.0)
+    first_stage(slice(192, 256), slice(32, 64))
+    for copy in halos[2]:
+        copy.wait_recv()
+    for part in range(2):
+        above = jnp.where(s > 0, from_prev[part, 0:32], 0.0)
+        below = jnp.where(s < scans - 1, from_next[part, 64:96], 0.0)
+        patch[part, 0:32] = jnp.where(seam >= offset, above, below)
+        patch[part, 64:96] = jnp.where(s > 0, from_prev[part, 64:96], 0.0)
+    first_stage(slice(0, 32), slice(64, 96))
+
     slices = [slice(i * CHUNK, (i + 1) * CHUNK) for i in range(CHUNKS)]
-    for rows in slices:
-        p_re, p_im = wave[0, rows], wave[1, rows]
-        o_re, o_im = patch[0, rows], patch[1, rows]
-        exit_wave = jnp.concatenate([p_re * o_re - p_im * o_im, p_re * o_im + p_im * o_re], axis=1)
-        keep(along_rows(exit_wave, 0), rows)
 
     def route(i):
         return (pair_a, pair_b) if i % 2 == 0 else (pair_b, pair_a)
 
     hops = []
     for i, rows in enumerate(slices):
-        f_re = along_columns(rows, 2)
-        f_im = along_columns(slice(PATCH + rows.start, PATCH + rows.stop), 2)
+        f_re, f_im = along_columns(i, 0)
         far[0, rows] = f_re
         far[1, rows] = f_im
         power[rows] = f_re * f_re + f_im * f_im
@@ -212,12 +276,11 @@
         intensity = power_sum[rows] + power_b[rows]
         factor = 1.0 - meas_ref[0, rows] / jnp.sqrt(jnp.maximum(intensity, 1.0))
         scaled = jnp.concatenate([far[0, rows] * factor, far[1, rows] * factor], axis=1)
-        keep(along_rows(scaled, 2), rows)
+        keep(along_rows(scaled, 1), rows)
 
     hops = []
     for i, rows in enumerate(slices):
-        b_re = along_columns(rows, 0)
-        b_im = along_columns(slice(PATCH + rows.start, PATCH + rows.stop), 0)
+        b_re, b_im = along_columns(i, 1)
         p_re, p_im = wave[0, rows], wave[1, rows]
         term[0, rows] = p_re * b_re + p_im * b_im
         term[1, rows] = p_re * b_im - p_im * b_re
@@ -303,14 +366,14 @@
     for inner in range(COLS // LANES):
         block = m * (COLS // LANES) + inner
         lanes = pl.ds(pl.multiple_of(lax.rem(block, 2) * LANES, LANES), LANES)
-        masks = [column_mask(corners[who, 0:1, :], block, shape) for who in range(3)]
+        masks = [column_mask(jnp.broadcast_to(corners[who, 0:1, :], shape), block, shape) for who in range(3)]
         for part in range(2):
             above = jnp.where(s > 0, grad_prev[part, :, lanes], 0.0)
             below = jnp.where(s < scans - 1, grad_next[part, :, lanes], 0.0)
             total = jnp.where(masks[1], total_term[part, ROWS : 2 * ROWS, lanes], 0.0)
             total = total + jnp.where(masks[0], above, 0.0) + jnp.where(masks[2], below, 0.0)
             here = slice(inner * LANES, (inner + 1) * LANES)
-            new_obj_ref[part, :, here] = obj_ref[part, :, here] - object_rate * total
+            new_obj_ref[part, :, here] = strip[m, part, :, here] - object_rate * total
 
     for copy in back_x:
         copy.wait_recv()
@@ -330,20 +393,26 @@
     chips_z = scans // (2 * chips_x)
     per_x = UNITS // chips_x
     per_z = per_x // chips_z
-    wire_count = 12 + 6 * CHUNKS // 2 + 4 + 2 + 2 * (chips_x + chips_z) + CHUNKS
+    wire_count = 28 + 6 * CHUNKS // 2 + 4 + 2 + 2 * (chips_x + chips_z) + CHUNKS
     field = pltpu.VMEM((2, PATCH, PATCH), F32)
     plane = pltpu.VMEM((PATCH, PATCH), F32)
     rim = pltpu.VMEM((2, ROWS, PATCH), F32)
     vmem = pl.BlockSpec(memory_space=pltpu.VMEM)
+    hbm = pl.BlockSpec(memory_space=pltpu.HBM)
     return pl.pallas_call(
         functools.partial(kernel, scans, chips_x, chips_z),
         out_shape=(
             jax.ShapeDtypeStruct(object_field.shape, F32),
             jax.ShapeDtypeStruct(probe.shape, F32),
         ),
-        in_specs=[pl.BlockSpec(memory_space=pltpu.SMEM)] + [vmem] * 4,
+        in_specs=[pl.BlockSpec(memory_space=pltpu.SMEM)] + [hbm] * 4,
         out_specs=(vmem, vmem),
         scratch_shapes=[
+            pltpu.VMEM(probe.shape, F32),
+            pltpu.VMEM(measured.shape, F32),
+            field,
+            pltpu.VMEM((2, 2, 2 * PATCH, 2 * PATCH), BF16),
+            pltpu.VMEM((2, 4 * PATCH, 2 * PATCH), BF16),
             pltpu.VMEM((MODES, 2, ROWS, COLS), F32),
             pltpu.VMEM((3, 8, LANES), jnp.int32),
             rim, rim, rim, rim,
@@ -362,12 +431,13 @@
             pltpu.VMEM((UNITS, 8, LANES), F32),
             pltpu.SemaphoreType.DMA((wire_count,)),
             pltpu.SemaphoreType.DMA((wire_count,)),
+            pltpu.SemaphoreType.DMA((4,)),
         ],
         compiler_params=pltpu.CompilerParams(
-            collective_id=0, has_side_effects=True, vmem_limit_bytes=48 << 20
+            collective_id=0, has_side_effects=True, vmem_limit_bytes=60 << 20
         ),
         cost_estimate=pl.CostEstimate(flops=1 << 31, bytes_accessed=4 << 20, transcendentals=0),
-    )(positions, object_field, probe, measured, jnp.asarray(dft_blocks()))
+    )(positions, object_field, probe, measured, jnp.asarray(dft_parts()))
 
 
 def solution(mesh):

time: 87.8 us -> 87.1 us (level)
  local copies, waits for them, and re-layouts: 6.7 us -> 2.55 us
  Pallas kernels: 80.2 us -> 83.8 us
    unnamed x12 -> x4, local copies, waits for them, and re-layouts: 6.7 us -> 2.55 us
    pallas_call x1, Pallas kernels: 80.2 us -> 83.8 us  [per_device(): pl.pallas_call(functools.partial(kernel, scans, chips_x, chips_z), out_sh...]
where the time goes in v2:
time: 87.1 us; the launch traced here: 87 us
  Pallas kernels  83.8 us (96%)
  local copies, waits for them, and re-layouts  2.55 us (3%)
    pallas_call x1, Pallas kernels, per_device(): pl.pallas_call(functools.partial(kernel, scans, chips_x, chips_z), out_sh...  83.8 us
    unnamed x4, local copies, waits for them, and re-layouts  2.55 us

profile of v2, /device:TPU:1, one launch (start us, length us, event | category | flops | bytes accessed | tf_op | source)
XLA Modules:
  0.0 87.0 jit_solution(4685127486253254376)
XLA Ops:
  0.6 83.8 %shard_map.68 = (f32[2,96,384]{2,1,0:T(8,128)}, f32[1,2,256,256]{3,2,1,0:T(8,128)}) custom-call(s32[1,2]{1,0:T(1,128)} %pos_ref.1, f32[2,96,384]{2,1,0:T(8,128)} %obj_ref.1, f32[1,2,256,256]{3,2,1,0:T(8,128)} %probe_hbm.1, f32[1,256,256]{2,1,0:T(8,128)} %meas_hbm.1, f32[2,256,256]{2,1,0:T(8,128)} %constant.2.clone.dft_hbm), custom_call_target="tpu_custom_call" | custom-call | flops 2147483648 | bytes 4194304 | tf_op jit(solution)/shard_map/pallas_call | solution.py:402
  84.4 0.0 copy-start
  84.4 1.8 %copy.9 = f32[2,96,384]{2,1,0:T(8,128)} copy(f32[2,96,384]{2,1,0:T(8,128)} %get-tuple-element.4) | data formatting | bytes 589824
  86.2 0.0 copy-done
  86.2 0.8 copy.10
Async XLA Ops:
  84.4 1.8 %copy-start = (f32[1,2,256,256]{3,2,1,0:T(8,128)S(1)}, f32[1,2,256,256]{3,2,1,0:T(8,128)}, u32[]{:S(2)}) copy-start(f32[1,2,256,256]{3,2,1,0:T(8,128)} %get-tuple-element.5) | copy-start | bytes 1572868

commit v3 on v2

v3 whole, which is shorter than its diff:
```python
import functools
import math

import jax
import jax.numpy as jnp
import ml_dtypes
import numpy as np
from jax import lax
from jax.experimental import pallas as pl
from jax.experimental.pallas import tpu as pltpu
from jax.sharding import PartitionSpec as P

MESH = pl.DeviceIdType.MESH
F32 = jnp.float32
BF16 = jnp.bfloat16
X_CHIPS = 4
MODES = 4
PATCH = 256
ROWS = 96
THIRD = 32
COLS = 384
LANES = 128
CHUNK = 64
SEAM = 32
CHUNKS = PATCH // CHUNK
object_rate = 0.25


def dft_parts():
    index = np.arange(PATCH)
    angle = 2.0 * math.pi / PATCH * (np.outer(index, index) % PATCH)
    scale = 1.0 / math.sqrt(PATCH)
    return np.stack([np.cos(angle) * scale, -np.sin(angle) * scale]).astype(np.float32)


def split(value):
    high = value.astype(BF16)
    return high, (value - high.astype(F32)).astype(BF16)


def dot(left, right):
    return jnp.dot(left, right, preferred_element_type=F32)


def column_mask(corner, block, shape):
    lane = lax.broadcasted_iota(jnp.int32, shape, 1) + block * LANES
    return (lane >= corner) & (lane < corner + PATCH)


def loop(count, body, start=0):
    def step(i, carry):
        body(i)
        return carry

    lax.fori_loop(start, count, step, 0)


def tiles(start, size, unit=8):
    return pl.ds(pl.multiple_of(start, unit), size)


class Wires:
    def __init__(self, send, recv):
        self.send, self.recv, self.used, self.open = send, recv, 0, []

    def take(self, count):
        first = self.used
        self.used += count
        return first

    def copy(self, src, dst, scan, mode, slot):
        return pltpu.make_async_remote_copy(
            src_ref=src,
            dst_ref=dst,
            send_sem=self.send.at[slot],
            recv_sem=self.recv.at[slot],
            device_id=(scan, mode),
            device_id_type=MESH,
        )

    def put(self, src, dst, scan, mode):
        copy = self.copy(src, dst, scan, mode, self.take(1))
        copy.start()
        self.open.append(copy)
        return copy

    def drain(self):
        for copy in self.open:
            copy.wait_send()
        self.open = []


def kernel(
    scans, chips_x, chips_z,
    pos_ref, obj_ref, probe_hbm, meas_hbm, dft_hbm,
    new_obj_ref, new_probe_ref,
    probe_ref, meas_ref, dft_ref, row_ops, col_ops,
    strip, corners, pick_next, pick_prev, from_prev, from_next,
    patch, wave, double, stack, far, power, power_a, power_sum, power_b,
    term, term_a, term_sum, term_b, total_term, rim_up, rim_down, grad_prev, grad_next,
    pgrad, pcore, halves, parts_x, shard, parts_z, gathered, gathered_other,
    send_sem, recv_sem, local_sem,
):
    s = lax.axis_index("scan")
    m = lax.axis_index("mode")
    core = lax.rem(s, 2)
    z = lax.rem(lax.div(s, 2), chips_z)
    x = lax.div(s, 2 * chips_z)
    nxt, prv = lax.rem(s + 1, scans), lax.rem(s + scans - 1, scans)
    m_up, m_dn = lax.rem(m + 1, MODES), lax.rem(m + MODES - 1, MODES)
    pair_a = jnp.where(lax.rem(m, 2) == 0, m + 1, m - 1)
    pair_b = MODES - 1 - m
    other_core = jnp.where(core == 0, s + 1, s - 1)
    wires = Wires(send_sem, recv_sem)
    per_z = 2 * CHUNK // chips_z

    def at_x(step):
        return (lax.rem(x + step, chips_x) * chips_z + z) * 2 + core

    def at_z(step):
        return (x * chips_z + lax.rem(z + step, chips_z)) * 2 + core

    barrier = pltpu.get_barrier_semaphore()

    def greet(scan, mode):
        pl.semaphore_signal(barrier, inc=1, device_id=(scan, mode), device_id_type=MESH)

    greet(s, m_up)
    greet(s, m_dn)
    greet(nxt, m)
    greet(prv, m)
    loop(chips_x, lambda step: greet(at_x(step), m), 1)
    loop(chips_z, lambda step: greet(at_z(step), m), 1)
    pl.semaphore_wait(barrier, 2 + chips_x + chips_z)

    def cells_of(tile, part, t):
        return strip.at[tile, part, t * THIRD : (t + 1) * THIRD]

    def own_cells(part, t):
        return obj_ref.at[part, t * THIRD : (t + 1) * THIRD]

    up, dn, fwd_up, fwd_dn = {}, {}, {}, {}

    def send_own(t):
        up[0, t] = wires.put(own_cells(0, t), cells_of(m, 0, t), s, m_up)
        dn[1, t] = wires.put(own_cells(1, t), cells_of(m, 1, t), s, m_dn)
        up[1, t] = wires.put(own_cells(1, t), cells_of(m, 1, t), s, m_up)
        dn[0, t] = wires.put(own_cells(0, t), cells_of(m, 0, t), s, m_dn)

    def forward(t):
        up[0, t].wait_recv()
        fwd_up[t] = wires.put(cells_of(m_dn, 0, t), cells_of(m_dn, 0, t), s, m_up)
        dn[1, t].wait_recv()
        fwd_dn[t] = wires.put(cells_of(m_up, 1, t), cells_of(m_up, 1, t), s, m_dn)

    send_own(0)
    moves = [(obj_ref, strip.at[m]), (dft_hbm, dft_ref), (probe_hbm, probe_ref), (meas_hbm, meas_ref)]
    local = [pltpu.make_async_copy(src, dst, local_sem.at[i]) for i, (src, dst) in enumerate(moves)]
    for copy in local:
        copy.start()
    row_at = pos_ref[0, 0]
    col_at = pos_ref[0, 1]
    corners[1] = jnp.full((8, LANES), col_at, jnp.int32)
    pos_next = wires.put(corners.at[1], corners.at[0], nxt, m)
    pos_prev = wires.put(corners.at[1], corners.at[2], prv, m)
    send_own(1)
    send_own(2)
    for copy in local:
        copy.wait()
    offset = row_at - ROWS * s + ROWS
    turn = jnp.bitwise_and(col_at, PATCH - 1)

    def transforms(i):
        rows = tiles(i * CHUNK, CHUNK, CHUNK)
        low_rows = tiles(PATCH + i * CHUNK, CHUNK, CHUNK)
        for part, (re, im) in enumerate(zip(split(dft_ref[0, rows]), split(dft_ref[1, rows]))):
            at = i * 4 * CHUNK + 2 * part * CHUNK
            for which, sign in enumerate((im, -im)):
                row_ops[which, part, rows, 0:PATCH] = re
                row_ops[which, part, rows, PATCH:] = sign
                row_ops[which, part, low_rows, 0:PATCH] = -sign
                row_ops[which, part, low_rows, PATCH:] = re
                col_ops[which, tiles(at, CHUNK, CHUNK), 0:PATCH] = re
                col_ops[which, tiles(at, CHUNK, CHUNK), PATCH:] = -sign
                col_ops[which, tiles(at + CHUNK, CHUNK, CHUNK), 0:PATCH] = sign
                col_ops[which, tiles(at + CHUNK, CHUNK, CHUNK), PATCH:] = re

    loop(CHUNKS, transforms)
    forward(0)

    def window(part, start, down):
        value = double[part, tiles(start, CHUNK + SEAM, SEAM)]
        return pltpu.roll(value, down, 0)[SEAM:]

    def turn_probe(i):
        rows = tiles(i * CHUNK, CHUNK, CHUNK)
        for part in range(2):
            rolled = pltpu.roll(probe_ref[0, part, rows], turn, 1)
            double[part, rows] = rolled
            double[part, tiles(PATCH + i * CHUNK, CHUNK, CHUNK)] = rolled

    def align_probe(i):
        for part in range(2):
            wave[part, tiles(i * CHUNK, CHUNK, CHUNK)] = window(part, i * CHUNK, offset)

    loop(CHUNKS, turn_probe)
    loop(CHUNKS, align_probe)
    pos_next.wait_recv()
    pos_prev.wait_recv()

    def choose(t):
        for copy in (dn[0, t], fwd_up[t], up[1, t], fwd_dn[t]):
            copy.wait_recv()

        def pick(j):
            part = lax.div(j, THIRD // 8)
            row = t * THIRD + lax.rem(j, THIRD // 8) * 8
            rows = tiles(row, 8)
            picked = [[jnp.zeros((8, LANES), F32)] * 2 for who in range(3)]
            corner = [corners[who] for who in range(3)]
            for block in range(MODES * COLS // LANES):
                tile, inner = divmod(block, COLS // LANES)
                cells = strip[tile, part, rows, inner * LANES : (inner + 1) * LANES]
                for who in range(3):
                    mask = column_mask(corner[who], block, (8, LANES))
                    picked[who][block % 2] = jnp.where(mask, cells, picked[who][block % 2])
            for half in range(2):
                lanes = slice(half * LANES, (half + 1) * LANES)
                pick_prev[part, rows, lanes] = picked[0][half]
                patch[part, tiles(CHUNK + row, 8), lanes] = picked[1][half]
                pick_next[part, rows, lanes] = picked[2][half]

        loop(2 * THIRD // 8, pick)
        rows = slice(t * THIRD, (t + 1) * THIRD)
        return (
            wires.put(pick_next.at[:, rows], from_prev.at[:, rows], nxt, m),
            wires.put(pick_prev.at[:, rows], from_next.at[:, rows], prv, m),
        )

    def along_rows(value, which):
        high, low = split(value)
        count = value.shape[0]
        both = dot(jnp.concatenate([high, low], axis=0), row_ops[which, 0])
        return both[:count] + both[count:] + dot(high, row_ops[which, 1])

    def along_columns(i, which):
        at = i * 4 * CHUNK
        both = dot(col_ops[which, tiles(at, 4 * CHUNK, CHUNK)], stack[0])
        result = both[: 2 * CHUNK] + both[2 * CHUNK :]
        result = result + dot(col_ops[which, tiles(at, 2 * CHUNK, CHUNK)], stack[1])
        return result[:CHUNK], result[CHUNK:]

    def keep(value, i):
        high, low = split(value)
        for part in range(2):
            lanes = slice(part * PATCH, (part + 1) * PATCH)
            into = tiles(part * PATCH + i * CHUNK, CHUNK, CHUNK)
            stack[0, into] = high[:, lanes]
            stack[1, into] = low[:, lanes]

    def first_stage(i):
        i = lax.rem(i, CHUNKS)
        rows = tiles(i * CHUNK, CHUNK, CHUNK)
        p_re, p_im = wave[0, rows], wave[1, rows]
        o_re, o_im = patch[0, rows], patch[1, rows]
        exit_wave = jnp.concatenate([p_re * o_re - p_im * o_im, p_re * o_im + p_im * o_re], axis=1)
        keep(along_rows(exit_wave, 0), i)

    halos = [choose(0)]
    forward(1)
    halos.append(choose(1))
    forward(2)
    halos.append(choose(2))
    for halo in halos[:2]:
        for copy in halo:
            copy.wait_recv()
    for part in range(2):
        patch[part, 160:224] = jnp.where(s < scans - 1, from_next[part, 0:64], 0.0)
    loop(3, first_stage, 1)
    seam = lax.broadcasted_iota(jnp.int32, (SEAM, PATCH), 0)
    for copy in halos[2]:
        copy.wait_recv()
    for part in range(2):
        above = jnp.where(s > 0, from_prev[part, 0:32], 0.0)
        below = jnp.where(s < scans - 1, from_next[part, 64:96], 0.0)
        patch[part, 224:256] = jnp.where(seam >= offset, above, below)
        patch[part, 0:64] = jnp.where(s > 0, from_prev[part, 32:96], 0.0)
    loop(5, first_stage, 3)

    def chunk_of(i):
        return tiles(i * CHUNK, CHUNK, CHUNK)

    def route(i):
        even = lax.rem(i, 2) == 0
        return jnp.where(even, pair_a, pair_b), jnp.where(even, pair_b, pair_a)

    power_slot = wires.take(2 * CHUNKS)

    def power_hop(i, second):
        rows = chunk_of(i)
        src, dst = (power_sum, power_b) if second else (power, power_a)
        slot = power_slot + second * CHUNKS + i
        return wires.copy(src.at[rows], dst.at[rows], s, route(i)[second], slot)

    def to_far(i):
        rows = chunk_of(i)
        f_re, f_im = along_columns(i, 0)
        far[0, rows] = f_re
        far[1, rows] = f_im
        power[rows] = f_re * f_re + f_im * f_im
        power_hop(i, 0).start()

    def add_power(i):
        rows = chunk_of(i)
        power_hop(i, 0).wait_recv()
        power_sum[rows] = power[rows] + power_a[rows]
        power_hop(i, 1).start()

    def rescale(i):
        rows = chunk_of(i)
        power_hop(i, 1).wait_recv()
        intensity = power_sum[rows] + power_b[rows]
        factor = 1.0 - meas_ref[0, rows] / jnp.sqrt(jnp.maximum(intensity, 1.0))
        scaled = jnp.concatenate([far[0, rows] * factor, far[1, rows] * factor], axis=1)
        keep(along_rows(scaled, 1), i)

    loop(CHUNKS, to_far)
    wires.drain()
    loop(CHUNKS, add_power)
    loop(CHUNKS, rescale)

    term_slot = wires.take(2 * CHUNKS)
    core_slot = wires.take(2 * CHUNKS)

    def nth(j):
        return lax.rem(x + j, CHUNKS)

    def term_hop(j, second):
        rows = chunk_of(nth(j))
        src, dst = (term_sum, term_b) if second else (term, term_a)
        slot = term_slot + second * CHUNKS + j
        return wires.copy(src.at[:, rows], dst.at[:, rows], s, route(j)[second], slot)

    def core_hop(j):
        n = nth(j)
        return wires.copy(pgrad.at[1 - core, n], pcore.at[n], other_core, m, core_slot + j - 1)

    def send_probe_terms(j):
        n = nth(j)
        for part in range(2):
            value = window(part, n * CHUNK + PATCH - SEAM, SEAM - offset)
            pgrad[part, n, 0:CHUNK] = value[:, :LANES]
            pgrad[part, n, CHUNK:] = value[:, LANES:]
        core_hop(j).start()

    def to_object(j):
        i = nth(j)
        rows = chunk_of(i)
        b_re, b_im = along_columns(i, 1)
        p_re, p_im = wave[0, rows], wave[1, rows]
        term[0, rows] = p_re * b_re + p_im * b_im
        term[1, rows] = p_re * b_im - p_im * b_re
        term_hop(j, 0).start()
        o_re, o_im = patch[0, rows], patch[1, rows]
        for part, value in enumerate((o_re * b_re + o_im * b_im, o_re * b_im - o_im * b_re)):
            value = pltpu.roll(value, PATCH - turn, 1)
            double[part, rows] = value
            double[part, tiles(PATCH + i * CHUNK, CHUNK, CHUNK)] = value

        @pl.when(j > 0)
        def _():
            send_probe_terms(j)

    loop(CHUNKS, to_object)
    send_probe_terms(CHUNKS)

    x_slot = wires.take(chips_x)
    back_x_slot = wires.take(chips_x)
    z_slot = wires.take(chips_z)
    back_z_slot = wires.take(chips_z)

    def x_hop(j):
        return wires.copy(halves.at[nth(j)], parts_x.at[j], at_x(j), m, x_slot + j)

    def add_core(j):
        n = nth(j)
        core_hop(j).wait_recv()
        halves[n] = pgrad[core, n] + pcore[n]

    def add_core_and_send(j):
        add_core(j)
        x_hop(j).start()

    loop(chips_x, add_core_and_send, 1)
    add_core(CHUNKS)

    def add_term(j):
        rows = chunk_of(nth(j))
        term_hop(j, 0).wait_recv()
        term_sum[:, rows] = term[:, rows] + term_a[:, rows]
        term_hop(j, 1).start()

    loop(CHUNKS, add_term)
    for j in range(1, chips_x):
        x_hop(j).wait_recv()
    total = halves[x]
    for j in range(1, chips_x):
        total = total + parts_x[j]
    shard[...] = total

    def z_rows(at):
        return tiles(at * per_z, per_z)

    def z_hop(j):
        there = z_rows(lax.rem(z + j, chips_z))
        return wires.copy(shard.at[there], parts_z.at[j], at_z(j), m, z_slot + j)

    loop(chips_z, lambda j: z_hop(j).start(), 1)
    loop(CHUNKS, lambda i: (power_hop(i, 0).wait_send(), power_hop(i, 1).wait_send()))

    def add_z(j, total):
        z_hop(j).wait_recv()
        return total + parts_z[j]

    total = lax.fori_loop(1, chips_z, add_z, shard[z_rows(z)])
    first = z * per_z
    half = lax.div(first, CHUNK) if per_z <= CHUNK else 0
    scale = 1.0 / math.sqrt(scans)
    old_rows = tiles(x * CHUNK + lax.rem(first, CHUNK), per_z)
    old = probe_ref[0, core, old_rows, tiles(half * LANES, LANES, LANES)]
    gathered[x, z_rows(z)] = old - total * scale

    def back_z_hop(j):
        mine = gathered.at[x, z_rows(z)]
        return wires.copy(mine, mine, at_z(j), m, back_z_slot + j)

    loop(chips_z, lambda j: back_z_hop(j).start(), 1)

    def total_terms(j):
        rows = chunk_of(nth(j))
        term_hop(j, 1).wait_recv()
        total_term[:, rows] = term_sum[:, rows] + term_b[:, rows]

    loop(CHUNKS, total_terms)
    for part in range(2):
        edge = total_term[part, 224:256]
        rim_up[part, 0:32] = jnp.where(seam >= offset, edge, 0.0)
        rim_up[part, 32:96] = total_term[part, 0:64]
        rim_down[part, 0:64] = total_term[part, 160:224]
        rim_down[part, 64:96] = jnp.where(seam < offset, edge, 0.0)
    to_prev = wires.put(rim_up, grad_next, prv, m)
    to_next = wires.put(rim_down, grad_prev, nxt, m)

    loop(chips_z, lambda j: back_z_hop(j).wait_recv(), 1)

    def back_x_hop(j):
        mine = gathered.at[x]
        return wires.copy(mine, mine, at_x(j), m, back_x_slot + j)

    def back_core_hop(j):
        mine = nth(CHUNKS - j)
        return wires.copy(gathered.at[mine], gathered_other.at[mine], other_core, m, core_slot + CHUNKS + j)

    loop(chips_x, lambda j: back_x_hop(j).start(), 1)
    back_core_hop(0).start()

    loop(CHUNKS, lambda j: (term_hop(j, 0).wait_send(), term_hop(j, 1).wait_send()))
    loop(CHUNKS + 1, lambda j: core_hop(j).wait_send(), 1)
    loop(chips_x, lambda j: x_hop(j).wait_send(), 1)
    loop(chips_z, lambda j: (z_hop(j).wait_send(), back_z_hop(j).wait_send()), 1)

    to_prev.wait_recv()
    to_next.wait_recv()
    shape = (ROWS, LANES)
    for inner in range(COLS // LANES):
        block = m * (COLS // LANES) + inner
        lanes = tiles(lax.rem(block, 2) * LANES, LANES, LANES)
        masks = [column_mask(jnp.broadcast_to(corners[who, 0:1, :], shape), block, shape) for who in range(3)]
        here = slice(inner * LANES, (inner + 1) * LANES)
        for part in range(2):
            above = jnp.where(s > 0, grad_prev[part, :, lanes], 0.0)
            below = jnp.where(s < scans - 1, grad_next[part, :, lanes], 0.0)
            total = jnp.where(masks[1], total_term[part, CHUNK : CHUNK + ROWS, lanes], 0.0)
            total = total + jnp.where(masks[0], above, 0.0) + jnp.where(masks[2], below, 0.0)
            new_obj_ref[part, :, here] = strip[m, part, :, here] - object_rate * total
    wires.drain()

    def pass_on(j):
        back_x_hop(j).wait_recv()
        back_core_hop(j).start()

    loop(chips_x, pass_on, 1)

    def put_probe(which, source, n):
        rows = chunk_of(n)
        new_probe_ref[0, which, rows, 0:LANES] = source[n, 0:CHUNK]
        new_probe_ref[0, which, rows, LANES:] = source[n, CHUNK:]

    loop(CHUNKS, lambda n: put_probe(core, gathered, n))

    def take_core(j):
        back_core_hop(j).wait_recv()
        put_probe(1 - core, gathered_other, nth(CHUNKS - j))

    loop(CHUNKS, take_core)
    loop(CHUNKS, lambda j: back_core_hop(j).wait_send())
    loop(chips_x, lambda j: back_x_hop(j).wait_send(), 1)


def per_device(scans, chips_x, object_field, probe, measured, positions):
    chips_z = scans // (2 * chips_x)
    per_z = 2 * CHUNK // chips_z
    wire_count = 28 + 6 * CHUNKS + 2 * (chips_x + chips_z)
    field = pltpu.VMEM((2, PATCH, PATCH), F32)
    plane = pltpu.VMEM((PATCH, PATCH), F32)
    rim = pltpu.VMEM((2, ROWS, PATCH), F32)
    share = pltpu.VMEM((CHUNKS, 2 * CHUNK, LANES), F32)
    vmem = pl.BlockSpec(memory_space=pltpu.VMEM)
    hbm = pl.BlockSpec(memory_space=pltpu.HBM)
    return pl.pallas_call(
        functools.partial(kernel, scans, chips_x, chips_z),
        out_shape=(
            jax.ShapeDtypeStruct(object_field.shape, F32),
            jax.ShapeDtypeStruct(probe.shape, F32),
        ),
        in_specs=[pl.BlockSpec(memory_space=pltpu.SMEM)] + [hbm] * 4,
        out_specs=(vmem, vmem),
        scratch_shapes=[
            pltpu.VMEM(probe.shape, F32),
            pltpu.VMEM(measured.shape, F32),
            field,
            pltpu.VMEM((2, 2, 2 * PATCH, 2 * PATCH), BF16),
            pltpu.VMEM((2, 4 * PATCH, 2 * PATCH), BF16),
            pltpu.VMEM((MODES, 2, ROWS, COLS), F32),
            pltpu.VMEM((3, 8, LANES), jnp.int32),
            rim, rim, rim, rim,
            field, field,
            pltpu.VMEM((2, 2 * PATCH, PATCH), F32),
            pltpu.VMEM((2, 2 * PATCH, PATCH), BF16),
            field,
            plane, plane, plane, plane,
            field, field, field, field, field,
            rim, rim, rim, rim,
            pltpu.VMEM((2, CHUNKS, 2 * CHUNK, LANES), F32),
            share, share, share,
            pltpu.VMEM((2 * CHUNK, LANES), F32),
            pltpu.VMEM((chips_z, per_z, LANES), F32),
            share, share,
            pltpu.SemaphoreType.DMA((wire_count,)),
            pltpu.SemaphoreType.DMA((wire_count,)),
            pltpu.SemaphoreType.DMA((4,)),
        ],
        compiler_params=pltpu.CompilerParams(
            collective_id=0, has_side_effects=True, vmem_limit_bytes=60 << 20
        ),
        cost_estimate=pl.CostEstimate(flops=1 << 31, bytes_accessed=4 << 20, transcendentals=0),
    )(positions, object_field, probe, measured, jnp.asarray(dft_parts()))


def solution(mesh):
    return jax.shard_map(
        functools.partial(per_device, mesh.shape["scan"], X_CHIPS),
        mesh=mesh,
        in_specs=(
            P(None, "scan", "mode"),
            P("mode", None, None, None),
            P("scan", None, None),
            P("scan", None),
        ),
        out_specs=(P(None, "scan", "mode"), P("mode", None, None, None)),
        check_vma=False,
    )
```

time: 87.1 us -> 86.7 us (level)
  no operation moved by 1% of the time
where the time goes in v3:
time: 86.7 us; the launch traced here: 86.5 us
  Pallas kernels  83.3 us (96%)
  local copies, waits for them, and re-layouts  2.55 us (3%)
    pallas_call x1, Pallas kernels, per_device(): pl.pallas_call(functools.partial(kernel, scans, chips_x, chips_z), out_sh...  83.3 us
    unnamed x4, local copies, waits for them, and re-layouts  2.55 us

profile of v3, /device:TPU:1, one launch (start us, length us, event | category | flops | bytes accessed | tf_op | source)
XLA Modules:
  0.0 86.5 jit_solution(9250676158593399188)
XLA Ops:
  0.6 83.3 %shard_map.68 = (f32[2,96,384]{2,1,0:T(8,128)}, f32[1,2,256,256]{3,2,1,0:T(8,128)}) custom-call(s32[1,2]{1,0:T(1,128)} %pos_ref.1, f32[2,96,384]{2,1,0:T(8,128)} %obj_ref.1, f32[1,2,256,256]{3,2,1,0:T(8,128)} %probe_hbm.1, f32[1,256,256]{2,1,0:T(8,128)} %meas_hbm.1, f32[2,256,256]{2,1,0:T(8,128)} %constant.2.clone.dft_hbm), custom_call_target="tpu_custom_call" | custom-call | flops 2147483648 | bytes 4194304 | tf_op jit(solution)/shard_map/pallas_call | solution.py:520
  84.0 0.0 copy-start
  84.0 1.8 %copy.9 = f32[2,96,384]{2,1,0:T(8,128)} copy(f32[2,96,384]{2,1,0:T(8,128)} %get-tuple-element.4) | data formatting | bytes 589824
  85.8 0.0 copy-done
  85.8 0.8 copy.10
Async XLA Ops:
  84.0 1.8 %copy-start = (f32[1,2,256,256]{3,2,1,0:T(8,128)S(1)}, f32[1,2,256,256]{3,2,1,0:T(8,128)}, u32[]{:S(2)}) copy-start(f32[1,2,256,256]{3,2,1,0:T(8,128)} %get-tuple-element.5) | copy-start | bytes 1572868

commit v4 on v3

--- a/solution.py
+++ b/solution.py
@@ -93,13 +93,13 @@
 def kernel(
     scans, chips_x, chips_z,
     pos_ref, obj_ref, probe_hbm, meas_hbm, dft_hbm,
-    new_obj_ref, new_probe_ref,
+    obj_out, probe_out,
     probe_ref, meas_ref, dft_ref, row_ops, col_ops,
     strip, corners, pick_next, pick_prev, from_prev, from_next,
     patch, wave, double, stack, far, power, power_a, power_sum, power_b,
     term, term_a, term_sum, term_b, total_term, rim_up, rim_down, grad_prev, grad_next,
     pgrad, pcore, halves, parts_x, shard, parts_z, gathered, gathered_other,
-    send_sem, recv_sem, local_sem,
+    new_obj, send_sem, recv_sem, local_sem, out_sem,
 ):
     s = lax.axis_index("scan")
     m = lax.axis_index("mode")
@@ -374,13 +374,20 @@
     loop(CHUNKS, to_object)
     send_probe_terms(CHUNKS)
 
-    x_slot = wires.take(chips_x)
-    back_x_slot = wires.take(chips_x)
+    x_slot = wires.take(2 * chips_x)
+    back_x_slot = wires.take(2 * chips_x)
     z_slot = wires.take(chips_z)
     back_z_slot = wires.take(chips_z)
 
-    def x_hop(j):
-        return wires.copy(halves.at[nth(j)], parts_x.at[j], at_x(j), m, x_slot + j)
+    block_z = max(chips_z // 2, 1)
+    blocks = chips_z // block_z
+
+    def block_rows(b):
+        return pl.ds(b * block_z * per_z, block_z * per_z)
+
+    def x_hop(j, b):
+        rows = block_rows(b)
+        return wires.copy(halves.at[nth(j), rows], parts_x.at[j, rows], at_x(j), m, x_slot + 2 * j + b)
 
     def add_core(j):
         n = nth(j)
@@ -389,9 +396,11 @@
 
     def add_core_and_send(j):
         add_core(j)
-        x_hop(j).start()
+        x_hop(j, 0).start()
 
     loop(chips_x, add_core_and_send, 1)
+    for b in range(1, blocks):
+        loop(chips_x, lambda j: x_hop(j, b).start(), 1)
     add_core(CHUNKS)
 
     def add_term(j):
@@ -401,13 +410,6 @@
         term_hop(j, 1).start()
 
     loop(CHUNKS, add_term)
-    for j in range(1, chips_x):
-        x_hop(j).wait_recv()
-    total = halves[x]
-    for j in range(1, chips_x):
-        total = total + parts_x[j]
-    shard[...] = total
-
     def z_rows(at):
         return tiles(at * per_z, per_z)
 
@@ -415,7 +417,23 @@
         there = z_rows(lax.rem(z + j, chips_z))
         return wires.copy(shard.at[there], parts_z.at[j], at_z(j), m, z_slot + j)
 
-    loop(chips_z, lambda j: z_hop(j).start(), 1)
+    for b in range(blocks):
+        rows = block_rows(b)
+        total = halves[x, rows]
+        for j in range(1, chips_x):
+            x_hop(j, b).wait_recv()
+            total = total + parts_x[j, rows]
+        shard[rows] = total
+
+        def send_z(i):
+            j = lax.rem(b * block_z + lax.rem(z + i, block_z) - z + chips_z, chips_z)
+
+            @pl.when(j > 0)
+            def _():
+                z_hop(j).start()
+
+        loop(block_z, send_z)
+
     loop(CHUNKS, lambda i: (power_hop(i, 0).wait_send(), power_hop(i, 1).wait_send()))
 
     def add_z(j, total):
@@ -451,22 +469,32 @@
     to_prev = wires.put(rim_up, grad_next, prv, m)
     to_next = wires.put(rim_down, grad_prev, nxt, m)
 
-    loop(chips_z, lambda j: back_z_hop(j).wait_recv(), 1)
-
-    def back_x_hop(j):
-        mine = gathered.at[x]
-        return wires.copy(mine, mine, at_x(j), m, back_x_slot + j)
+    def back_x_hop(j, b):
+        mine = gathered.at[x, block_rows(b)]
+        return wires.copy(mine, mine, at_x(j), m, back_x_slot + 2 * j + b)
+
+    for b in range(blocks):
+
+        def take_z(i):
+            j = lax.rem(z - b * block_z - i + chips_z, chips_z)
+
+            @pl.when(j > 0)
+            def _():
+                back_z_hop(j).wait_recv()
+
+        loop(block_z, take_z)
+        loop(chips_x, lambda j: back_x_hop(j, b).start(), 1)
 
     def back_core_hop(j):
         mine = nth(CHUNKS - j)
         return wires.copy(gathered.at[mine], gathered_other.at[mine], other_core, m, core_slot + CHUNKS + j)
 
-    loop(chips_x, lambda j: back_x_hop(j).start(), 1)
     back_core_hop(0).start()
 
     loop(CHUNKS, lambda j: (term_hop(j, 0).wait_send(), term_hop(j, 1).wait_send()))
     loop(CHUNKS + 1, lambda j: core_hop(j).wait_send(), 1)
-    loop(chips_x, lambda j: x_hop(j).wait_send(), 1)
+    for b in range(blocks):
+        loop(chips_x, lambda j: x_hop(j, b).wait_send(), 1)
     loop(chips_z, lambda j: (z_hop(j).wait_send(), back_z_hop(j).wait_send()), 1)
 
     to_prev.wait_recv()
@@ -482,49 +510,88 @@
             below = jnp.where(s < scans - 1, grad_next[part, :, lanes], 0.0)
             total = jnp.where(masks[1], total_term[part, CHUNK : CHUNK + ROWS, lanes], 0.0)
             total = total + jnp.where(masks[0], above, 0.0) + jnp.where(masks[2], below, 0.0)
-            new_obj_ref[part, :, here] = strip[m, part, :, here] - object_rate * total
+            new_obj[part, :, here] = strip[m, part, :, here] - object_rate * total
+    obj_copy = pltpu.make_async_copy(new_obj, obj_out, out_sem.at[0])
+    obj_copy.start()
     wires.drain()
 
+    def probe_copy(which, source, n, half, slot):
+        return pltpu.make_async_copy(
+            source.at[n, half * CHUNK : (half + 1) * CHUNK],
+            probe_out.at[0, which, chunk_of(n), half * LANES : (half + 1) * LANES],
+            out_sem.at[slot],
+        )
+
+    def mine_copy(j, half):
+        return probe_copy(core, gathered, nth(CHUNKS - j), half, 1 + 2 * j + half)
+
+    def other_copy(j, half):
+        return probe_copy(1 - core, gathered_other, nth(CHUNKS - j), half, 1 + 2 * (CHUNKS + j) + half)
+
+    def put_both(copy, j):
+        copy(j, 0).start()
+        copy(j, 1).start()
+
+    def wait_both(copy, j):
+        copy(j, 0).wait()
+        copy(j, 1).wait()
+
+    put_both(mine_copy, 0)
+
     def pass_on(j):
-        back_x_hop(j).wait_recv()
+        for b in range(blocks):
+            back_x_hop(j, b).wait_recv()
         back_core_hop(j).start()
+        put_both(mine_copy, j)
 
     loop(chips_x, pass_on, 1)
-
-    def put_probe(which, source, n):
-        rows = chunk_of(n)
-        new_probe_ref[0, which, rows, 0:LANES] = source[n, 0:CHUNK]
-        new_probe_ref[0, which, rows, LANES:] = source[n, CHUNK:]
-
-    loop(CHUNKS, lambda n: put_probe(core, gathered, n))
 
     def take_core(j):
         back_core_hop(j).wait_recv()
-        put_probe(1 - core, gathered_other, nth(CHUNKS - j))
+        put_both(other_copy, j)
 
     loop(CHUNKS, take_core)
     loop(CHUNKS, lambda j: back_core_hop(j).wait_send())
-    loop(chips_x, lambda j: back_x_hop(j).wait_send(), 1)
+    for b in range(blocks):
+        loop(chips_x, lambda j: back_x_hop(j, b).wait_send(), 1)
+    obj_copy.wait()
+    loop(CHUNKS, lambda j: (wait_both(mine_copy, j), wait_both(other_copy, j)))
+
+
+PIECES = 4
+
+
+def placing(obj_in, probe_in, obj_out, probe_out, sem):
+    copies = []
+    for src, dst, dim in ((obj_in, obj_out, 1), (probe_in, probe_out, 2)):
+        size = src.shape[dim] // PIECES
+        for i in range(PIECES):
+            where = (slice(None),) * dim + (slice(i * size, (i + 1) * size),)
+            copies.append(pltpu.make_async_copy(src.at[where], dst.at[where], sem.at[len(copies)]))
+    for copy in copies:
+        copy.start()
+    for copy in copies:
+        copy.wait()
 
 
 def per_device(scans, chips_x, object_field, probe, measured, positions):
     chips_z = scans // (2 * chips_x)
     per_z = 2 * CHUNK // chips_z
-    wire_count = 28 + 6 * CHUNKS + 2 * (chips_x + chips_z)
+    wire_count = 28 + 6 * CHUNKS + 4 * chips_x + 2 * chips_z
     field = pltpu.VMEM((2, PATCH, PATCH), F32)
     plane = pltpu.VMEM((PATCH, PATCH), F32)
     rim = pltpu.VMEM((2, ROWS, PATCH), F32)
     share = pltpu.VMEM((CHUNKS, 2 * CHUNK, LANES), F32)
-    vmem = pl.BlockSpec(memory_space=pltpu.VMEM)
     hbm = pl.BlockSpec(memory_space=pltpu.HBM)
-    return pl.pallas_call(
+    out_shape = (
+        jax.ShapeDtypeStruct(object_field.shape, F32),
+        jax.ShapeDtypeStruct(probe.shape, F32),
+    )
+    results = pl.pallas_call(
         functools.partial(kernel, scans, chips_x, chips_z),
-        out_shape=(
-            jax.ShapeDtypeStruct(object_field.shape, F32),
-            jax.ShapeDtypeStruct(probe.shape, F32),
-        ),
+        out_shape=out_shape,
         in_specs=[pl.BlockSpec(memory_space=pltpu.SMEM)] + [hbm] * 4,
-        out_specs=(vmem, vmem),
+        out_specs=(hbm, hbm),
         scratch_shapes=[
             pltpu.VMEM(probe.shape, F32),
             pltpu.VMEM(measured.shape, F32),
@@ -546,15 +613,25 @@
             pltpu.VMEM((2 * CHUNK, LANES), F32),
             pltpu.VMEM((chips_z, per_z, LANES), F32),
             share, share,
+            pltpu.VMEM(object_field.shape, F32),
             pltpu.SemaphoreType.DMA((wire_count,)),
             pltpu.SemaphoreType.DMA((wire_count,)),
             pltpu.SemaphoreType.DMA((4,)),
+            pltpu.SemaphoreType.DMA((1 + 4 * CHUNKS,)),
         ],
         compiler_params=pltpu.CompilerParams(
             collective_id=0, has_side_effects=True, vmem_limit_bytes=60 << 20
         ),
         cost_estimate=pl.CostEstimate(flops=1 << 31, bytes_accessed=4 << 20, transcendentals=0),
     )(positions, object_field, probe, measured, jnp.asarray(dft_parts()))
+    return pl.pallas_call(
+        placing,
+        out_shape=out_shape,
+        in_specs=[hbm, hbm],
+        out_specs=(hbm, hbm),
+        scratch_shapes=[pltpu.SemaphoreType.DMA((2 * PIECES,))],
+        compiler_params=pltpu.CompilerParams(vmem_limit_bytes=60 << 20),
+    )(*results)
 
 
 def solution(mesh):

time: 86.7 us -> 109 us (1.26)
  Pallas kernels: 83.3 us -> 108 us
  local copies, waits for them, and re-layouts: 2.55 us -> 0 us
    pallas_call x0 -> x1, Pallas kernels: none -> 26 us  [per_device(): pl.pallas_call(placing, out_shape=out_shape, in_specs=[hbm, hbm], out_spe...]
    unnamed x4 -> x0, local copies, waits for them, and re-layouts: 2.55 us -> none
where the time goes in v4:
time: 109 us
  Pallas kernels  108 us (99%)
    pallas_call x1, Pallas kernels, per_device(): pl.pallas_call(functools.partial(kernel, scans, chips_x, chips_z), out_sh...  82.4 us
    pallas_call x1, Pallas kernels, per_device(): pl.pallas_call(placing, out_shape=out_shape, in_specs=[hbm, hbm], out_spe...  26 us

profile of v4, /device:TPU:1, one launch (start us, length us, event | category | flops | bytes accessed | tf_op | source)
XLA Modules:
  0.0 109.0 jit_solution(5734340988256866857)
XLA Ops:
  0.6 82.4 %shard_map.68 = (f32[2,96,384]{2,1,0:T(8,128)}, f32[1,2,256,256]{3,2,1,0:T(8,128)}) custom-call(s32[1,2]{1,0:T(1,128)} %pos_ref.1, f32[2,96,384]{2,1,0:T(8,128)} %obj_ref.1, f32[1,2,256,256]{3,2,1,0:T(8,128)} %probe_hbm.1, f32[1,256,256]{2,1,0:T(8,128)} %meas_hbm.1, f32[2,256,256]{2,1,0:T(8,128)} %constant.2.clone.dft_hbm), custom_call_target="tpu_custom_call" | custom-call | flops 2147483648 | bytes 4194304 | tf_op jit(solution)/shard_map/pallas_call | solution.py:590
  83.0 26.0 %shard_map.69 = (f32[2,96,384]{2,1,0:T(8,128)}, f32[1,2,256,256]{3,2,1,0:T(8,128)}) custom-call(f32[2,96,384]{2,1,0:T(8,128)} %get-tuple-element.4.obj_in, f32[1,2,256,256]{3,2,1,0:T(8,128)} %get-tuple-element.5.probe_in), custom_call_target="tpu_custom_call" | custom-call | tf_op jit(solution)/shard_map/pallas_call | solution.py:627

commit v5 on v4

--- a/solution.py
+++ b/solution.py
@@ -120,6 +120,10 @@
     def at_z(step):
         return (x * chips_z + lax.rem(z + step, chips_z)) * 2 + core
 
+    moves = [(obj_ref, strip.at[m]), (dft_hbm, dft_ref), (probe_hbm, probe_ref), (meas_hbm, meas_ref)]
+    local = [pltpu.make_async_copy(src, dst, local_sem.at[i]) for i, (src, dst) in enumerate(moves)]
+    for copy in local:
+        copy.start()
     barrier = pltpu.get_barrier_semaphore()
 
     def greet(scan, mode):
@@ -136,16 +140,13 @@
     def cells_of(tile, part, t):
         return strip.at[tile, part, t * THIRD : (t + 1) * THIRD]
 
-    def own_cells(part, t):
-        return obj_ref.at[part, t * THIRD : (t + 1) * THIRD]
-
     up, dn, fwd_up, fwd_dn = {}, {}, {}, {}
 
     def send_own(t):
-        up[0, t] = wires.put(own_cells(0, t), cells_of(m, 0, t), s, m_up)
-        dn[1, t] = wires.put(own_cells(1, t), cells_of(m, 1, t), s, m_dn)
-        up[1, t] = wires.put(own_cells(1, t), cells_of(m, 1, t), s, m_up)
-        dn[0, t] = wires.put(own_cells(0, t), cells_of(m, 0, t), s, m_dn)
+        up[0, t] = wires.put(cells_of(m, 0, t), cells_of(m, 0, t), s, m_up)
+        dn[1, t] = wires.put(cells_of(m, 1, t), cells_of(m, 1, t), s, m_dn)
+        up[1, t] = wires.put(cells_of(m, 1, t), cells_of(m, 1, t), s, m_up)
+        dn[0, t] = wires.put(cells_of(m, 0, t), cells_of(m, 0, t), s, m_dn)
 
     def forward(t):
         up[0, t].wait_recv()
@@ -153,11 +154,8 @@
         dn[1, t].wait_recv()
         fwd_dn[t] = wires.put(cells_of(m_up, 1, t), cells_of(m_up, 1, t), s, m_dn)
 
+    local[0].wait()
     send_own(0)
-    moves = [(obj_ref, strip.at[m]), (dft_hbm, dft_ref), (probe_hbm, probe_ref), (meas_hbm, meas_ref)]
-    local = [pltpu.make_async_copy(src, dst, local_sem.at[i]) for i, (src, dst) in enumerate(moves)]
-    for copy in local:
-        copy.start()
     row_at = pos_ref[0, 0]
     col_at = pos_ref[0, 1]
     corners[1] = jnp.full((8, LANES), col_at, jnp.int32)
@@ -165,7 +163,7 @@
     pos_prev = wires.put(corners.at[1], corners.at[2], prv, m)
     send_own(1)
     send_own(2)
-    for copy in local:
+    for copy in local[1:]:
         copy.wait()
     offset = row_at - ROWS * s + ROWS
     turn = jnp.bitwise_and(col_at, PATCH - 1)
@@ -409,7 +407,6 @@
         term_sum[:, rows] = term[:, rows] + term_a[:, rows]
         term_hop(j, 1).start()
 
-    loop(CHUNKS, add_term)
     def z_rows(at):
         return tiles(at * per_z, per_z)
 
@@ -417,7 +414,9 @@
         there = z_rows(lax.rem(z + j, chips_z))
         return wires.copy(shard.at[there], parts_z.at[j], at_z(j), m, z_slot + j)
 
+    per_block = CHUNKS // blocks
     for b in range(blocks):
+        loop((b + 1) * per_block, add_term, b * per_block)
         rows = block_rows(b)
         total = halves[x, rows]
         for j in range(1, chips_x):
@@ -453,6 +452,28 @@
         return wires.copy(mine, mine, at_z(j), m, back_z_slot + j)
 
     loop(chips_z, lambda j: back_z_hop(j).start(), 1)
+
+    def back_x_hop(j, b):
+        mine = gathered.at[x, block_rows(b)]
+        return wires.copy(mine, mine, at_x(j), m, back_x_slot + 2 * j + b)
+
+    for b in range(blocks):
+
+        def take_z(i):
+            j = lax.rem(z - b * block_z - i + chips_z, chips_z)
+
+            @pl.when(j > 0)
+            def _():
+                back_z_hop(j).wait_recv()
+
+        loop(block_z, take_z)
+        loop(chips_x, lambda j: back_x_hop(j, b).start(), 1)
+
+    def back_core_hop(j):
+        mine = nth(CHUNKS - j)
+        return wires.copy(gathered.at[mine], gathered_other.at[mine], other_core, m, core_slot + CHUNKS + j)
+
+    back_core_hop(0).start()
 
     def total_terms(j):
         rows = chunk_of(nth(j))
@@ -469,33 +490,42 @@
     to_prev = wires.put(rim_up, grad_next, prv, m)
     to_next = wires.put(rim_down, grad_prev, nxt, m)
 
-    def back_x_hop(j, b):
-        mine = gathered.at[x, block_rows(b)]
-        return wires.copy(mine, mine, at_x(j), m, back_x_slot + 2 * j + b)
-
-    for b in range(blocks):
-
-        def take_z(i):
-            j = lax.rem(z - b * block_z - i + chips_z, chips_z)
-
-            @pl.when(j > 0)
-            def _():
-                back_z_hop(j).wait_recv()
-
-        loop(block_z, take_z)
-        loop(chips_x, lambda j: back_x_hop(j, b).start(), 1)
-
-    def back_core_hop(j):
-        mine = nth(CHUNKS - j)
-        return wires.copy(gathered.at[mine], gathered_other.at[mine], other_core, m, core_slot + CHUNKS + j)
-
-    back_core_hop(0).start()
-
     loop(CHUNKS, lambda j: (term_hop(j, 0).wait_send(), term_hop(j, 1).wait_send()))
     loop(CHUNKS + 1, lambda j: core_hop(j).wait_send(), 1)
     for b in range(blocks):
         loop(chips_x, lambda j: x_hop(j, b).wait_send(), 1)
     loop(chips_z, lambda j: (z_hop(j).wait_send(), back_z_hop(j).wait_send()), 1)
+
+    def probe_copy(which, source, n, half, slot):
+        return pltpu.make_async_copy(
+            source.at[n, half * CHUNK : (half + 1) * CHUNK],
+            probe_out.at[0, which, chunk_of(n), half * LANES : (half + 1) * LANES],
+            out_sem.at[slot],
+        )
+
+    def mine_copy(j, half):
+        return probe_copy(core, gathered, nth(CHUNKS - j), half, 1 + 2 * j + half)
+
+    def other_copy(j, half):
+        return probe_copy(1 - core, gathered_other, nth(CHUNKS - j), half, 1 + 2 * (CHUNKS + j) + half)
+
+    def put_both(copy, j):
+        copy(j, 0).start()
+        copy(j, 1).start()
+
+    def wait_both(copy, j):
+        copy(j, 0).wait()
+        copy(j, 1).wait()
+
+    put_both(mine_copy, 0)
+
+    def pass_on(j):
+        for b in range(blocks):
+            back_x_hop(j, b).wait_recv()
+        back_core_hop(j).start()
+        put_both(mine_copy, j)
+
+    loop(chips_x, pass_on, 1)
 
     to_prev.wait_recv()
     to_next.wait_recv()
@@ -515,37 +545,6 @@
     obj_copy.start()
     wires.drain()
 
-    def probe_copy(which, source, n, half, slot):
-        return pltpu.make_async_copy(
-            source.at[n, half * CHUNK : (half + 1) * CHUNK],
-            probe_out.at[0, which, chunk_of(n), half * LANES : (half + 1) * LANES],
-            out_sem.at[slot],
-        )
-
-    def mine_copy(j, half):
-        return probe_copy(core, gathered, nth(CHUNKS - j), half, 1 + 2 * j + half)
-
-    def other_copy(j, half):
-        return probe_copy(1 - core, gathered_other, nth(CHUNKS - j), half, 1 + 2 * (CHUNKS + j) + half)
-
-    def put_both(copy, j):
-        copy(j, 0).start()
-        copy(j, 1).start()
-
-    def wait_both(copy, j):
-        copy(j, 0).wait()
-        copy(j, 1).wait()
-
-    put_both(mine_copy, 0)
-
-    def pass_on(j):
-        for b in range(blocks):
-            back_x_hop(j, b).wait_recv()
-        back_core_hop(j).start()
-        put_both(mine_copy, j)
-
-    loop(chips_x, pass_on, 1)
-
     def take_core(j):
         back_core_hop(j).wait_recv()
         put_both(other_copy, j)
@@ -561,17 +560,22 @@
 PIECES = 4
 
 
-def placing(obj_in, probe_in, obj_out, probe_out, sem):
-    copies = []
-    for src, dst, dim in ((obj_in, obj_out, 1), (probe_in, probe_out, 2)):
+def placing(obj_in, probe_in, obj_out, probe_out, obj_held, probe_held, into, out):
+    pieces = []
+    for src, held, dst, dim in ((obj_in, obj_held, obj_out, 1), (probe_in, probe_held, probe_out, 2)):
         size = src.shape[dim] // PIECES
         for i in range(PIECES):
-            where = (slice(None),) * dim + (slice(i * size, (i + 1) * size),)
-            copies.append(pltpu.make_async_copy(src.at[where], dst.at[where], sem.at[len(copies)]))
-    for copy in copies:
-        copy.start()
-    for copy in copies:
-        copy.wait()
+            at = (slice(None),) * dim + (slice(i * size, (i + 1) * size),)
+            slot = len(pieces)
+            first = pltpu.make_async_copy(src.at[at], held.at[at], into.at[slot])
+            pieces.append((first, pltpu.make_async_copy(held.at[at], dst.at[at], out.at[slot])))
+    for first, second in pieces:
+        first.start()
+    for first, second in pieces:
+        first.wait()
+        second.start()
+    for first, second in pieces:
+        second.wait()
 
 
 def per_device(scans, chips_x, object_field, probe, measured, positions):
@@ -629,7 +633,12 @@
         out_shape=out_shape,
         in_specs=[hbm, hbm],
         out_specs=(hbm, hbm),
-        scratch_shapes=[pltpu.SemaphoreType.DMA((2 * PIECES,))],
+        scratch_shapes=[
+            pltpu.VMEM(object_field.shape, F32),
+            pltpu.VMEM(probe.shape, F32),
+            pltpu.SemaphoreType.DMA((2 * PIECES,)),
+            pltpu.SemaphoreType.DMA((2 * PIECES,)),
+        ],
         compiler_params=pltpu.CompilerParams(vmem_limit_bytes=60 << 20),
     )(*results)
 

time: 109 us -> 83 us (0.76)
  Pallas kernels: 108 us -> 82.2 us
    pallas_call x1, Pallas kernels: 26 us -> 2.02 us  [per_device(): pl.pallas_call(placing, out_shape=out_shape, in_specs=[hbm, hbm], out_spe...]
    pallas_call x1, Pallas kernels: 82.4 us -> 80.2 us  [per_device(): pl.pallas_call(functools.partial(kernel, scans, chips_x, chips_z), out_sh...]
where the time goes in v5:
time: 83 us; the launch traced here: 82.8 us
  Pallas kernels  82.2 us (99%)
    pallas_call x1, Pallas kernels, per_device(): pl.pallas_call(functools.partial(kernel, scans, chips_x, chips_z), out_sh...  80.2 us
    pallas_call x1, Pallas kernels, per_device(): pl.pallas_call(placing, out_shape=out_shape, in_specs=[hbm, hbm], out_spe...  2.02 us

profile of v5, /device:TPU:1, one launch (start us, length us, event | category | flops | bytes accessed | tf_op | source)
XLA Modules:
  0.0 82.8 jit_solution(11163102153935341426)
XLA Ops:
  0.6 80.2 %shard_map.68 = (f32[2,96,384]{2,1,0:T(8,128)}, f32[1,2,256,256]{3,2,1,0:T(8,128)}) custom-call(s32[1,2]{1,0:T(1,128)} %pos_ref.1, f32[2,96,384]{2,1,0:T(8,128)} %obj_ref.1, f32[1,2,256,256]{3,2,1,0:T(8,128)} %probe_hbm.1, f32[1,256,256]{2,1,0:T(8,128)} %meas_hbm.1, f32[2,256,256]{2,1,0:T(8,128)} %constant.2.clone.dft_hbm), custom_call_target="tpu_custom_call" | custom-call | flops 2147483648 | bytes 4194304 | tf_op jit(solution)/shard_map/pallas_call | solution.py:594
  80.8 2.0 %shard_map.69 = (f32[2,96,384]{2,1,0:T(8,128)}, f32[1,2,256,256]{3,2,1,0:T(8,128)}) custom-call(f32[2,96,384]{2,1,0:T(8,128)} %get-tuple-element.4.obj_in, f32[1,2,256,256]{3,2,1,0:T(8,128)} %get-tuple-element.5.probe_in), custom_call_target="tpu_custom_call" | custom-call | tf_op jit(solution)/shard_map/pallas_call | solution.py:631

commit v6 on v5

--- a/solution.py
+++ b/solution.py
@@ -99,7 +99,7 @@
     patch, wave, double, stack, far, power, power_a, power_sum, power_b,
     term, term_a, term_sum, term_b, total_term, rim_up, rim_down, grad_prev, grad_next,
     pgrad, pcore, halves, parts_x, shard, parts_z, gathered, gathered_other,
-    new_obj, send_sem, recv_sem, local_sem, out_sem,
+    new_obj, send_sem, recv_sem, local_sem, out_sem, token_sem_x, token_sem_z,
 ):
     s = lax.axis_index("scan")
     m = lax.axis_index("mode")
@@ -133,9 +133,36 @@
     greet(s, m_dn)
     greet(nxt, m)
     greet(prv, m)
-    loop(chips_x, lambda step: greet(at_x(step), m), 1)
-    loop(chips_z, lambda step: greet(at_z(step), m), 1)
-    pl.semaphore_wait(barrier, 2 + chips_x + chips_z)
+    near_x = sorted({1, chips_x - 1})
+    near_z = sorted({1, chips_z - 1})
+    for step in near_x:
+        greet(at_x(step), m)
+    for step in near_z:
+        greet(at_z(step), m)
+    pl.semaphore_wait(barrier, 4 + len(near_x) + len(near_z))
+
+    rounds_x = chips_x // 2 - 1
+    rounds_z = chips_z // 2 - 1
+
+    def send_token(sem, at, near, turn):
+        for way, step in enumerate(near):
+            pl.semaphore_signal(sem.at[turn, way], inc=1, device_id=(at(step), m), device_id_type=MESH)
+
+    def take_token(sem, near, turn):
+        for way in range(len(near)):
+            pl.semaphore_wait(sem.at[turn, way], 1)
+
+    def token_z(turn):
+        if 0 < turn <= rounds_z:
+            take_token(token_sem_z, near_z, turn - 1)
+        if turn < rounds_z:
+            send_token(token_sem_z, at_z, near_z, turn)
+
+    def token_x(turn):
+        if 0 < turn <= rounds_x:
+            take_token(token_sem_x, near_x, turn - 1)
+        if turn < rounds_x:
+            send_token(token_sem_x, at_x, near_x, turn)
 
     def cells_of(tile, part, t):
         return strip.at[tile, part, t * THIRD : (t + 1) * THIRD]
@@ -163,6 +190,8 @@
     pos_prev = wires.put(corners.at[1], corners.at[2], prv, m)
     send_own(1)
     send_own(2)
+    token_x(0)
+    token_z(0)
     for copy in local[1:]:
         copy.wait()
     offset = row_at - ROWS * s + ROWS
@@ -184,6 +213,7 @@
                 col_ops[which, tiles(at + CHUNK, CHUNK, CHUNK), PATCH:] = re
 
     loop(CHUNKS, transforms)
+    token_z(1)
     forward(0)
 
     def window(part, start, down):
@@ -203,8 +233,13 @@
 
     loop(CHUNKS, turn_probe)
     loop(CHUNKS, align_probe)
+    token_z(2)
+    forward(1)
     pos_next.wait_recv()
     pos_prev.wait_recv()
+    token_z(3)
+    forward(2)
+    token_z(4)
 
     def choose(t):
         for copy in (dn[0, t], fwd_up[t], up[1, t], fwd_dn[t]):
@@ -264,11 +299,8 @@
         exit_wave = jnp.concatenate([p_re * o_re - p_im * o_im, p_re * o_im + p_im * o_re], axis=1)
         keep(along_rows(exit_wave, 0), i)
 
-    halos = [choose(0)]
-    forward(1)
-    halos.append(choose(1))
-    forward(2)
-    halos.append(choose(2))
+    halos = [choose(0), choose(1), choose(2)]
+    token_z(5)
     for halo in halos[:2]:
         for copy in halo:
             copy.wait_recv()
@@ -323,8 +355,11 @@
         keep(along_rows(scaled, 1), i)
 
     loop(CHUNKS, to_far)
+    token_z(6)
     wires.drain()
     loop(CHUNKS, add_power)
+    token_z(7)
+    token_x(1)
     loop(CHUNKS, rescale)
 
     term_slot = wires.take(2 * CHUNKS)
@@ -371,6 +406,8 @@
 
     loop(CHUNKS, to_object)
     send_probe_terms(CHUNKS)
+
+    assert rounds_x <= 1 and rounds_z <= 7
 
     x_slot = wires.take(2 * chips_x)
     back_x_slot = wires.take(2 * chips_x)
@@ -622,6 +659,8 @@
             pltpu.SemaphoreType.DMA((wire_count,)),
             pltpu.SemaphoreType.DMA((4,)),
             pltpu.SemaphoreType.DMA((1 + 4 * CHUNKS,)),
+            pltpu.SemaphoreType.REGULAR((max(chips_x // 2 - 1, 1), 2)),
+            pltpu.SemaphoreType.REGULAR((max(chips_z // 2 - 1, 1), 2)),
         ],
         compiler_params=pltpu.CompilerParams(
             collective_id=0, has_side_effects=True, vmem_limit_bytes=60 << 20

time: 83 us -> 74.4 us (0.90)
  Pallas kernels: 82.2 us -> 72.8 us
    pallas_call x1, Pallas kernels: 80.2 us -> 70.8 us  [per_device(): pl.pallas_call(functools.partial(kernel, scans, chips_x, chips_z), out_sh...]
where the time goes in v6:
time: 74.4 us; the launch traced here: 73.5 us
  Pallas kernels  72.8 us (98%)
    pallas_call x1, Pallas kernels, per_device(): pl.pallas_call(functools.partial(kernel, scans, chips_x, chips_z), out_sh...  70.8 us
    pallas_call x1, Pallas kernels, per_device(): pl.pallas_call(placing, out_shape=out_shape, in_specs=[hbm, hbm], out_spe...  2.02 us

profile of v6, /device:TPU:1, one launch (start us, length us, event | category | flops | bytes accessed | tf_op | source)
XLA Modules:
  0.0 73.5 jit_solution(7522515513024954833)
XLA Ops:
  0.6 70.8 %shard_map.68 = (f32[2,96,384]{2,1,0:T(8,128)}, f32[1,2,256,256]{3,2,1,0:T(8,128)}) custom-call(s32[1,2]{1,0:T(1,128)} %pos_ref.1, f32[2,96,384]{2,1,0:T(8,128)} %obj_ref.1, f32[1,2,256,256]{3,2,1,0:T(8,128)} %probe_hbm.1, f32[1,256,256]{2,1,0:T(8,128)} %meas_hbm.1, f32[2,256,256]{2,1,0:T(8,128)} %constant.2.clone.dft_hbm), custom_call_target="tpu_custom_call" | custom-call | flops 2147483648 | bytes 4194304 | tf_op jit(solution)/shard_map/pallas_call | solution.py:631
  71.4 2.0 %shard_map.69 = (f32[2,96,384]{2,1,0:T(8,128)}, f32[1,2,256,256]{3,2,1,0:T(8,128)}) custom-call(f32[2,96,384]{2,1,0:T(8,128)} %get-tuple-element.4.obj_in, f32[1,2,256,256]{3,2,1,0:T(8,128)} %get-tuple-element.5.probe_in), custom_call_target="tpu_custom_call" | custom-call | tf_op jit(solution)/shard_map/pallas_call | solution.py:670

commit v7 on v6

--- a/solution.py
+++ b/solution.py
@@ -17,7 +17,7 @@
 MODES = 4
 PATCH = 256
 ROWS = 96
-THIRD = 32
+BANDS = ((0, 40), (40, 80), (80, 96))
 COLS = 384
 LANES = 128
 CHUNK = 64
@@ -99,7 +99,7 @@
     patch, wave, double, stack, far, power, power_a, power_sum, power_b,
     term, term_a, term_sum, term_b, total_term, rim_up, rim_down, grad_prev, grad_next,
     pgrad, pcore, halves, parts_x, shard, parts_z, gathered, gathered_other,
-    new_obj, send_sem, recv_sem, local_sem, out_sem, token_sem_x, token_sem_z,
+    ordered, new_obj, send_sem, recv_sem, local_sem, out_sem, token_sem_x, token_sem_z,
 ):
     s = lax.axis_index("scan")
     m = lax.axis_index("mode")
@@ -165,7 +165,7 @@
             send_token(token_sem_x, at_x, near_x, turn)
 
     def cells_of(tile, part, t):
-        return strip.at[tile, part, t * THIRD : (t + 1) * THIRD]
+        return strip.at[tile, part, slice(*BANDS[t])]
 
     up, dn, fwd_up, fwd_dn = {}, {}, {}, {}
 
@@ -213,7 +213,6 @@
                 col_ops[which, tiles(at + CHUNK, CHUNK, CHUNK), PATCH:] = re
 
     loop(CHUNKS, transforms)
-    token_z(1)
     forward(0)
 
     def window(part, start, down):
@@ -233,21 +232,22 @@
 
     loop(CHUNKS, turn_probe)
     loop(CHUNKS, align_probe)
-    token_z(2)
     forward(1)
+    token_z(1)
     pos_next.wait_recv()
     pos_prev.wait_recv()
-    token_z(3)
     forward(2)
-    token_z(4)
+    token_z(2)
 
     def choose(t):
         for copy in (dn[0, t], fwd_up[t], up[1, t], fwd_dn[t]):
             copy.wait_recv()
 
+        count = (BANDS[t][1] - BANDS[t][0]) // 8
+
         def pick(j):
-            part = lax.div(j, THIRD // 8)
-            row = t * THIRD + lax.rem(j, THIRD // 8) * 8
+            part = lax.div(j, count)
+            row = BANDS[t][0] + lax.rem(j, count) * 8
             rows = tiles(row, 8)
             picked = [[jnp.zeros((8, LANES), F32)] * 2 for who in range(3)]
             corner = [corners[who] for who in range(3)]
@@ -263,8 +263,8 @@
                 patch[part, tiles(CHUNK + row, 8), lanes] = picked[1][half]
                 pick_next[part, rows, lanes] = picked[2][half]
 
-        loop(2 * THIRD // 8, pick)
-        rows = slice(t * THIRD, (t + 1) * THIRD)
+        loop(2 * count, pick)
+        rows = slice(*BANDS[t])
         return (
             wires.put(pick_next.at[:, rows], from_prev.at[:, rows], nxt, m),
             wires.put(pick_prev.at[:, rows], from_next.at[:, rows], prv, m),
@@ -299,8 +299,10 @@
         exit_wave = jnp.concatenate([p_re * o_re - p_im * o_im, p_re * o_im + p_im * o_re], axis=1)
         keep(along_rows(exit_wave, 0), i)
 
-    halos = [choose(0), choose(1), choose(2)]
-    token_z(5)
+    halos = []
+    for t in range(3):
+        halos.append(choose(t))
+        token_z(3 + t)
     for halo in halos[:2]:
         for copy in halo:
             copy.wait_recv()
@@ -393,7 +395,6 @@
         p_re, p_im = wave[0, rows], wave[1, rows]
         term[0, rows] = p_re * b_re + p_im * b_im
         term[1, rows] = p_re * b_im - p_im * b_re
-        term_hop(j, 0).start()
         o_re, o_im = patch[0, rows], patch[1, rows]
         for part, value in enumerate((o_re * b_re + o_im * b_im, o_re * b_im - o_im * b_re)):
             value = pltpu.roll(value, PATCH - turn, 1)
@@ -406,28 +407,49 @@
 
     loop(CHUNKS, to_object)
     send_probe_terms(CHUNKS)
+    loop(CHUNKS // 2, lambda j: term_hop(j, 0).start())
 
     assert rounds_x <= 1 and rounds_z <= 7
 
-    x_slot = wires.take(2 * chips_x)
-    back_x_slot = wires.take(2 * chips_x)
+
+    block_z = max(chips_z // 4, 1)
+    blocks = chips_z // block_z
+    order = sorted(range(chips_z), key=lambda step: -min(step, chips_z - step))
+
+    def piece(i):
+        return slice(i * per_z, (i + 1) * per_z)
+
+    def piece_z(i):
+        return lax.rem(z + order[i], chips_z)
+
+    def distance(i):
+        return order[i]
+
+    def opposite(i):
+        return order.index((chips_z - order[i]) % chips_z)
+
+    mine_at = order.index(0)
+    x_slot = wires.take(blocks * chips_x)
+    back_x_slot = wires.take(blocks * chips_x)
     z_slot = wires.take(chips_z)
     back_z_slot = wires.take(chips_z)
 
-    block_z = max(chips_z // 2, 1)
-    blocks = chips_z // block_z
-
     def block_rows(b):
         return pl.ds(b * block_z * per_z, block_z * per_z)
 
     def x_hop(j, b):
         rows = block_rows(b)
-        return wires.copy(halves.at[nth(j), rows], parts_x.at[j, rows], at_x(j), m, x_slot + 2 * j + b)
+        return wires.copy(halves.at[nth(j), rows], parts_x.at[j, rows], at_x(j), m, x_slot + blocks * j + b)
+
+    def z_rows(at):
+        return tiles(at * per_z, per_z)
 
     def add_core(j):
         n = nth(j)
         core_hop(j).wait_recv()
-        halves[n] = pgrad[core, n] + pcore[n]
+        for i in range(chips_z):
+            rows = z_rows(piece_z(i))
+            halves[n, piece(i)] = pgrad[core, n, rows] + pcore[n, rows]
 
     def add_core_and_send(j):
         add_core(j)
@@ -436,6 +458,7 @@
     loop(chips_x, add_core_and_send, 1)
     for b in range(1, blocks):
         loop(chips_x, lambda j: x_hop(j, b).start(), 1)
+    loop(CHUNKS, lambda j: term_hop(j, 0).start(), CHUNKS // 2)
     add_core(CHUNKS)
 
     def add_term(j):
@@ -444,16 +467,14 @@
         term_sum[:, rows] = term[:, rows] + term_a[:, rows]
         term_hop(j, 1).start()
 
-    def z_rows(at):
-        return tiles(at * per_z, per_z)
-
-    def z_hop(j):
-        there = z_rows(lax.rem(z + j, chips_z))
-        return wires.copy(shard.at[there], parts_z.at[j], at_z(j), m, z_slot + j)
-
-    per_block = CHUNKS // blocks
+    def z_hop(i):
+        j = distance(i)
+        return wires.copy(shard.at[piece(i)], parts_z.at[j], at_z(j), m, z_slot + j)
+
+    others = [i for i in range(chips_z) if i != mine_at]
+
+    loop(CHUNKS // 2, add_term)
     for b in range(blocks):
-        loop((b + 1) * per_block, add_term, b * per_block)
         rows = block_rows(b)
         total = halves[x, rows]
         for j in range(1, chips_x):
@@ -461,69 +482,64 @@
             total = total + parts_x[j, rows]
         shard[rows] = total
 
-        def send_z(i):
-            j = lax.rem(b * block_z + lax.rem(z + i, block_z) - z + chips_z, chips_z)
-
-            @pl.when(j > 0)
-            def _():
-                z_hop(j).start()
-
-        loop(block_z, send_z)
-
+        for i in (i for i in others if i // block_z == b):
+            z_hop(i).start()
+
+    loop(CHUNKS, add_term, CHUNKS // 2)
     loop(CHUNKS, lambda i: (power_hop(i, 0).wait_send(), power_hop(i, 1).wait_send()))
 
-    def add_z(j, total):
-        z_hop(j).wait_recv()
-        return total + parts_z[j]
-
-    total = lax.fori_loop(1, chips_z, add_z, shard[z_rows(z)])
+    total = shard[piece(mine_at)]
+    for i in reversed(others):
+        z_hop(i).wait_recv()
+        total = total + parts_z[distance(i)]
     first = z * per_z
     half = lax.div(first, CHUNK) if per_z <= CHUNK else 0
     scale = 1.0 / math.sqrt(scans)
     old_rows = tiles(x * CHUNK + lax.rem(first, CHUNK), per_z)
     old = probe_ref[0, core, old_rows, tiles(half * LANES, LANES, LANES)]
-    gathered[x, z_rows(z)] = old - total * scale
-
-    def back_z_hop(j):
-        mine = gathered.at[x, z_rows(z)]
-        return wires.copy(mine, mine, at_z(j), m, back_z_slot + j)
-
-    loop(chips_z, lambda j: back_z_hop(j).start(), 1)
+    gathered[x, piece(mine_at)] = old - total * scale
+
+    def back_z_hop(i):
+        j = distance(i)
+        there = piece(opposite(i))
+        src = gathered.at[x, piece(mine_at)]
+        return wires.copy(src, gathered.at[x, there], at_z(j), m, back_z_slot + j)
+
+    for i in others:
+        back_z_hop(i).start()
 
     def back_x_hop(j, b):
         mine = gathered.at[x, block_rows(b)]
-        return wires.copy(mine, mine, at_x(j), m, back_x_slot + 2 * j + b)
-
-    for b in range(blocks):
-
-        def take_z(i):
-            j = lax.rem(z - b * block_z - i + chips_z, chips_z)
-
-            @pl.when(j > 0)
-            def _():
-                back_z_hop(j).wait_recv()
-
-        loop(block_z, take_z)
-        loop(chips_x, lambda j: back_x_hop(j, b).start(), 1)
-
-    def back_core_hop(j):
-        mine = nth(CHUNKS - j)
-        return wires.copy(gathered.at[mine], gathered_other.at[mine], other_core, m, core_slot + CHUNKS + j)
-
-    back_core_hop(0).start()
+        return wires.copy(mine, mine, at_x(j), m, back_x_slot + blocks * j + b)
 
     def total_terms(j):
         rows = chunk_of(nth(j))
         term_hop(j, 1).wait_recv()
         total_term[:, rows] = term_sum[:, rows] + term_b[:, rows]
 
-    loop(CHUNKS, total_terms)
-    for part in range(2):
-        edge = total_term[part, 224:256]
-        rim_up[part, 0:32] = jnp.where(seam >= offset, edge, 0.0)
-        rim_up[part, 32:96] = total_term[part, 0:64]
-        rim_down[part, 0:64] = total_term[part, 160:224]
-        rim_down[part, 64:96] = jnp.where(seam < offset, edge, 0.0)
+    def make_rims():
+        loop(CHUNKS, total_terms)
+        for part in range(2):
+            edge = total_term[part, 224:256]
+            rim_up[part, 0:32] = jnp.where(seam >= offset, edge, 0.0)
+            rim_up[part, 32:96] = total_term[part, 0:64]
+            rim_down[part, 0:64] = total_term[part, 160:224]
+            rim_down[part, 64:96] = jnp.where(seam < offset, edge, 0.0)
+
+    for b in reversed(range(blocks)):
+        for i in others:
+            if opposite(i) // block_z == b:
+                back_z_hop(i).wait_recv()
+        loop(chips_x, lambda j: back_x_hop(j, b).start(), 1)
+        if b == max(blocks - 2, 0):
+            make_rims()
+
+    def back_core_hop(j):
+        mine = nth(CHUNKS - j)
+        return wires.copy(gathered.at[mine], gathered_other.at[mine], other_core, m, core_slot + CHUNKS + j)
+
+    back_core_hop(0).start()
+
     to_prev = wires.put(rim_up, grad_next, prv, m)
     to_next = wires.put(rim_down, grad_prev, nxt, m)
 
@@ -531,7 +547,9 @@
     loop(CHUNKS + 1, lambda j: core_hop(j).wait_send(), 1)
     for b in range(blocks):
         loop(chips_x, lambda j: x_hop(j, b).wait_send(), 1)
-    loop(chips_z, lambda j: (z_hop(j).wait_send(), back_z_hop(j).wait_send()), 1)
+    for i in others:
+        z_hop(i).wait_send()
+        back_z_hop(i).wait_send()
 
     def probe_copy(which, source, n, half, slot):
         return pltpu.make_async_copy(
@@ -541,12 +559,16 @@
         )
 
     def mine_copy(j, half):
-        return probe_copy(core, gathered, nth(CHUNKS - j), half, 1 + 2 * j + half)
+        return probe_copy(core, ordered.at[0], nth(CHUNKS - j), half, 1 + 2 * j + half)
 
     def other_copy(j, half):
-        return probe_copy(1 - core, gathered_other, nth(CHUNKS - j), half, 1 + 2 * (CHUNKS + j) + half)
-
-    def put_both(copy, j):
+        return probe_copy(1 - core, ordered.at[1], nth(CHUNKS - j), half, 1 + 2 * (CHUNKS + j) + half)
+
+    def put_both(copy, source, j):
+        n = nth(CHUNKS - j)
+        for i in range(chips_z):
+            ordered_rows = z_rows(piece_z(i))
+            ordered[source, n, ordered_rows] = (gathered, gathered_other)[source][n, piece(i)]
         copy(j, 0).start()
         copy(j, 1).start()
 
@@ -554,37 +576,47 @@
         copy(j, 0).wait()
         copy(j, 1).wait()
 
-    put_both(mine_copy, 0)
+    put_both(mine_copy, 0, 0)
+
+    def tile_part(inner):
+        shape = (ROWS, LANES)
+        block = m * (COLS // LANES) + inner
+        lanes = tiles(lax.rem(block, 2) * LANES, LANES, LANES)
+
+        def mask(who):
+            return column_mask(jnp.broadcast_to(corners[who, 0:1, :], shape), block, shape)
+
+        return slice(inner * LANES, (inner + 1) * LANES), lanes, mask
+
+    for inner in range(COLS // LANES):
+        here, lanes, mask = tile_part(inner)
+        for part in range(2):
+            own = jnp.where(mask(1), total_term[part, CHUNK : CHUNK + ROWS, lanes], 0.0)
+            new_obj[part, :, here] = strip[m, part, :, here] - object_rate * own
 
     def pass_on(j):
         for b in range(blocks):
             back_x_hop(j, b).wait_recv()
         back_core_hop(j).start()
-        put_both(mine_copy, j)
+        put_both(mine_copy, 0, j)
 
     loop(chips_x, pass_on, 1)
 
     to_prev.wait_recv()
     to_next.wait_recv()
-    shape = (ROWS, LANES)
     for inner in range(COLS // LANES):
-        block = m * (COLS // LANES) + inner
-        lanes = tiles(lax.rem(block, 2) * LANES, LANES, LANES)
-        masks = [column_mask(jnp.broadcast_to(corners[who, 0:1, :], shape), block, shape) for who in range(3)]
-        here = slice(inner * LANES, (inner + 1) * LANES)
+        here, lanes, mask = tile_part(inner)
         for part in range(2):
-            above = jnp.where(s > 0, grad_prev[part, :, lanes], 0.0)
-            below = jnp.where(s < scans - 1, grad_next[part, :, lanes], 0.0)
-            total = jnp.where(masks[1], total_term[part, CHUNK : CHUNK + ROWS, lanes], 0.0)
-            total = total + jnp.where(masks[0], above, 0.0) + jnp.where(masks[2], below, 0.0)
-            new_obj[part, :, here] = strip[m, part, :, here] - object_rate * total
+            above = jnp.where(mask(0) & (s > 0), grad_prev[part, :, lanes], 0.0)
+            below = jnp.where(mask(2) & (s < scans - 1), grad_next[part, :, lanes], 0.0)
+            new_obj[part, :, here] = new_obj[part, :, here] - object_rate * (above + below)
     obj_copy = pltpu.make_async_copy(new_obj, obj_out, out_sem.at[0])
     obj_copy.start()
     wires.drain()
 
     def take_core(j):
         back_core_hop(j).wait_recv()
-        put_both(other_copy, j)
+        put_both(other_copy, 1, j)
 
     loop(CHUNKS, take_core)
     loop(CHUNKS, lambda j: back_core_hop(j).wait_send())
@@ -597,33 +629,29 @@
 PIECES = 4
 
 
-def placing(obj_in, probe_in, obj_out, probe_out, obj_held, probe_held, into, out):
-    pieces = []
-    for src, held, dst, dim in ((obj_in, obj_held, obj_out, 1), (probe_in, probe_held, probe_out, 2)):
+def placing(obj_in, probe_in, obj_out, probe_out, sem):
+    copies = []
+    for src, dst, dim in ((obj_in, obj_out, 1), (probe_in, probe_out, 2)):
         size = src.shape[dim] // PIECES
         for i in range(PIECES):
             at = (slice(None),) * dim + (slice(i * size, (i + 1) * size),)
-            slot = len(pieces)
-            first = pltpu.make_async_copy(src.at[at], held.at[at], into.at[slot])
-            pieces.append((first, pltpu.make_async_copy(held.at[at], dst.at[at], out.at[slot])))
-    for first, second in pieces:
-        first.start()
-    for first, second in pieces:
-        first.wait()
-        second.start()
-    for first, second in pieces:
-        second.wait()
+            copies.append(pltpu.make_async_copy(src.at[at], dst.at[at], sem.at[len(copies)]))
+    for copy in copies:
+        copy.start()
+    for copy in copies:
+        copy.wait()
 
 
 def per_device(scans, chips_x, object_field, probe, measured, positions):
     chips_z = scans // (2 * chips_x)
     per_z = 2 * CHUNK // chips_z
-    wire_count = 28 + 6 * CHUNKS + 4 * chips_x + 2 * chips_z
+    wire_count = 28 + 6 * CHUNKS + 8 * chips_x + 2 * chips_z
     field = pltpu.VMEM((2, PATCH, PATCH), F32)
     plane = pltpu.VMEM((PATCH, PATCH), F32)
     rim = pltpu.VMEM((2, ROWS, PATCH), F32)
     share = pltpu.VMEM((CHUNKS, 2 * CHUNK, LANES), F32)
     hbm = pl.BlockSpec(memory_space=pltpu.HBM)
+    anywhere = pl.BlockSpec(memory_space=pl.ANY)
     out_shape = (
         jax.ShapeDtypeStruct(object_field.shape, F32),
         jax.ShapeDtypeStruct(probe.shape, F32),
@@ -632,7 +660,7 @@
         functools.partial(kernel, scans, chips_x, chips_z),
         out_shape=out_shape,
         in_specs=[pl.BlockSpec(memory_space=pltpu.SMEM)] + [hbm] * 4,
-        out_specs=(hbm, hbm),
+        out_specs=(anywhere, anywhere),
         scratch_shapes=[
             pltpu.VMEM(probe.shape, F32),
             pltpu.VMEM(measured.shape, F32),
@@ -654,6 +682,7 @@
             pltpu.VMEM((2 * CHUNK, LANES), F32),
             pltpu.VMEM((chips_z, per_z, LANES), F32),
             share, share,
+            pltpu.VMEM((2, CHUNKS, 2 * CHUNK, LANES), F32),
             pltpu.VMEM(object_field.shape, F32),
             pltpu.SemaphoreType.DMA((wire_count,)),
             pltpu.SemaphoreType.DMA((wire_count,)),
@@ -663,23 +692,20 @@
             pltpu.SemaphoreType.REGULAR((max(chips_z // 2 - 1, 1), 2)),
         ],
         compiler_params=pltpu.CompilerParams(
-            collective_id=0, has_side_effects=True, vmem_limit_bytes=60 << 20
+            collective_id=0, has_side_effects=True, vmem_limit_bytes=32 << 20
         ),
         cost_estimate=pl.CostEstimate(flops=1 << 31, bytes_accessed=4 << 20, transcendentals=0),
-    )(positions, object_field, probe, measured, jnp.asarray(dft_parts()))
+    )(*[
+        pltpu.with_memory_space_constraint(value, pltpu.HBM)
+        for value in (positions, object_field, probe, measured, jnp.asarray(dft_parts()))
+    ])
     return pl.pallas_call(
         placing,
         out_shape=out_shape,
-        in_specs=[hbm, hbm],
+        in_specs=[anywhere, anywhere],
         out_specs=(hbm, hbm),
-        scratch_shapes=[
-            pltpu.VMEM(object_field.shape, F32),
-            pltpu.VMEM(probe.shape, F32),
-            pltpu.SemaphoreType.DMA((2 * PIECES,)),
-            pltpu.SemaphoreType.DMA((2 * PIECES,)),
-        ],
-        compiler_params=pltpu.CompilerParams(vmem_limit_bytes=60 << 20),
-    )(*results)
+        scratch_shapes=[pltpu.SemaphoreType.DMA((2 * PIECES,))],
+    )(*[pltpu.with_memory_space_constraint(value, pltpu.VMEM) for value in results])
 
 
 def solution(mesh):

time: 74.4 us -> 72.4 us (0.973); the launches traced: 73.5 us -> 72.3 us
  Pallas kernels: 72.8 us -> 71.7 us
    pallas_call x1, Pallas kernels: 2.02 us -> 0.95 us  [per_device(): pl.pallas_call(placing, out_shape=out_shape, in_specs=[anywhere, anywhere...]
where the time goes in v7:
time: 72.4 us; the launch traced here: 72.3 us
  Pallas kernels  71.7 us (99%)
    pallas_call x1, Pallas kernels, per_device(): pl.pallas_call(functools.partial(kernel, scans, chips_x, chips_z), out_sh...  70.7 us

profile of v7, /device:TPU:1, one launch (start us, length us, event | category | flops | bytes accessed | tf_op | source)
XLA Modules:
  0.0 72.3 jit_solution(2165279518751268017)
XLA Ops:
  0.6 70.7 %shard_map.68 = (f32[2,96,384]{2,1,0:T(8,128)S(1)}, f32[1,2,256,256]{3,2,1,0:T(8,128)S(1)}) custom-call(s32[1,2]{1,0:T(1,128)} %pos_ref.1, f32[2,96,384]{2,1,0:T(8,128)} %obj_ref.1, f32[1,2,256,256]{3,2,1,0:T(8,128)} %probe_hbm.1, f32[1,256,256]{2,1,0:T(8,128)} %meas_hbm.1, f32[2,256,256]{2,1,0:T(8,128)} %constant.2.clone.dft_hbm), custom_call_target="tpu_custom_call" | custom-call | flops 2147483648 | bytes 4194304 | tf_op jit(solution)/shard_map/pallas_call | solution.py:659
  71.3 1.0 %shard_map.69 = (f32[2,96,384]{2,1,0:T(8,128)}, f32[1,2,256,256]{3,2,1,0:T(8,128)}) custom-call(f32[2,96,384]{2,1,0:T(8,128)S(1)} %get-tuple-element.4.obj_in, f32[1,2,256,256]{3,2,1,0:T(8,128)S(1)} %get-tuple-element.5.probe_in), custom_call_target="tpu_custom_call" | custom-call | tf_op jit(solution)/shard_map/pallas_call | solution.py:702

commit v8 on v7

--- a/solution.py
+++ b/solution.py
@@ -411,35 +411,35 @@
 
     assert rounds_x <= 1 and rounds_z <= 7
 
-
-    block_z = max(chips_z // 4, 1)
+    x_slot = wires.take(2 * chips_x)
+    back_x_slot = wires.take(2 * chips_x)
+    z_slot = wires.take(chips_z)
+    back_z_slot = wires.take(chips_z)
+
+    block_z = max(chips_z // 2, 1)
     blocks = chips_z // block_z
-    order = sorted(range(chips_z), key=lambda step: -min(step, chips_z - step))
+    quarter = chips_z // 4
 
     def piece(i):
         return slice(i * per_z, (i + 1) * per_z)
 
     def piece_z(i):
-        return lax.rem(z + order[i], chips_z)
+        return lax.rem(z + quarter + i, chips_z)
 
     def distance(i):
-        return order[i]
-
-    def opposite(i):
-        return order.index((chips_z - order[i]) % chips_z)
-
-    mine_at = order.index(0)
-    x_slot = wires.take(blocks * chips_x)
-    back_x_slot = wires.take(blocks * chips_x)
-    z_slot = wires.take(chips_z)
-    back_z_slot = wires.take(chips_z)
+        return (quarter + i) % chips_z
+
+    mine_at = (chips_z - quarter) % chips_z
+
+    def far_first(places):
+        return sorted(places, key=lambda i: -min(distance(i), chips_z - distance(i)))
 
     def block_rows(b):
         return pl.ds(b * block_z * per_z, block_z * per_z)
 
     def x_hop(j, b):
         rows = block_rows(b)
-        return wires.copy(halves.at[nth(j), rows], parts_x.at[j, rows], at_x(j), m, x_slot + blocks * j + b)
+        return wires.copy(halves.at[nth(j), rows], parts_x.at[j, rows], at_x(j), m, x_slot + 2 * j + b)
 
     def z_rows(at):
         return tiles(at * per_z, per_z)
@@ -482,14 +482,14 @@
             total = total + parts_x[j, rows]
         shard[rows] = total
 
-        for i in (i for i in others if i // block_z == b):
+        for i in far_first(i for i in others if i // block_z == b):
             z_hop(i).start()
 
     loop(CHUNKS, add_term, CHUNKS // 2)
     loop(CHUNKS, lambda i: (power_hop(i, 0).wait_send(), power_hop(i, 1).wait_send()))
 
     total = shard[piece(mine_at)]
-    for i in reversed(others):
+    for i in reversed(far_first(others)):
         z_hop(i).wait_recv()
         total = total + parts_z[distance(i)]
     first = z * per_z
@@ -501,16 +501,16 @@
 
     def back_z_hop(i):
         j = distance(i)
-        there = piece(opposite(i))
+        there = piece((mine_at - j) % chips_z)
         src = gathered.at[x, piece(mine_at)]
         return wires.copy(src, gathered.at[x, there], at_z(j), m, back_z_slot + j)
 
-    for i in others:
+    for i in far_first(others):
         back_z_hop(i).start()
 
     def back_x_hop(j, b):
         mine = gathered.at[x, block_rows(b)]
-        return wires.copy(mine, mine, at_x(j), m, back_x_slot + blocks * j + b)
+        return wires.copy(mine, mine, at_x(j), m, back_x_slot + 2 * j + b)
 
     def total_terms(j):
         rows = chunk_of(nth(j))
@@ -527,11 +527,11 @@
             rim_down[part, 64:96] = jnp.where(seam < offset, edge, 0.0)
 
     for b in reversed(range(blocks)):
-        for i in others:
-            if opposite(i) // block_z == b:
+        for i in range(chips_z):
+            if i != mine_at and (mine_at - distance(i)) % chips_z // block_z == b:
                 back_z_hop(i).wait_recv()
         loop(chips_x, lambda j: back_x_hop(j, b).start(), 1)
-        if b == max(blocks - 2, 0):
+        if b == blocks - 1:
             make_rims()
 
     def back_core_hop(j):
@@ -645,7 +645,7 @@
 def per_device(scans, chips_x, object_field, probe, measured, positions):
     chips_z = scans // (2 * chips_x)
     per_z = 2 * CHUNK // chips_z
-    wire_count = 28 + 6 * CHUNKS + 8 * chips_x + 2 * chips_z
+    wire_count = 28 + 6 * CHUNKS + 4 * chips_x + 2 * chips_z
     field = pltpu.VMEM((2, PATCH, PATCH), F32)
     plane = pltpu.VMEM((PATCH, PATCH), F32)
     rim = pltpu.VMEM((2, ROWS, PATCH), F32)

time: 72.4 us -> 72.1 us (level)
  no operation moved by 1% of the time
where the time goes in v8:
time: 72.1 us; the launch traced here: 72 us
  Pallas kernels  71.3 us (99%)
    pallas_call x1, Pallas kernels, per_device(): pl.pallas_call(functools.partial(kernel, scans, chips_x, chips_z), out_sh...  70.4 us

profile of v8, /device:TPU:1, one launch (start us, length us, event | category | flops | bytes accessed | tf_op | source)
XLA Modules:
  0.0 72.0 jit_solution(15566172670056648978)
XLA Ops:
  0.6 70.4 %shard_map.68 = (f32[2,96,384]{2,1,0:T(8,128)S(1)}, f32[1,2,256,256]{3,2,1,0:T(8,128)S(1)}) custom-call(s32[1,2]{1,0:T(1,128)} %pos_ref.1, f32[2,96,384]{2,1,0:T(8,128)} %obj_ref.1, f32[1,2,256,256]{3,2,1,0:T(8,128)} %probe_hbm.1, f32[1,256,256]{2,1,0:T(8,128)} %meas_hbm.1, f32[2,256,256]{2,1,0:T(8,128)} %constant.2.clone.dft_hbm), custom_call_target="tpu_custom_call" | custom-call | flops 2147483648 | bytes 4194304 | tf_op jit(solution)/shard_map/pallas_call | solution.py:659
  71.0 1.0 %shard_map.69 = (f32[2,96,384]{2,1,0:T(8,128)}, f32[1,2,256,256]{3,2,1,0:T(8,128)}) custom-call(f32[2,96,384]{2,1,0:T(8,128)S(1)} %get-tuple-element.4.obj_in, f32[1,2,256,256]{3,2,1,0:T(8,128)S(1)} %get-tuple-element.5.probe_in), custom_call_target="tpu_custom_call" | custom-call | tf_op jit(solution)/shard_map/pallas_call | solution.py:702
